TPU v7x, 512 devices: a whole 4x8x8 slice. The times are simulated.
512 devices in a mesh: rows: 128 (over z, y, core), rep: 4 (over x).
Axes of the slice: x: 4, y: 8, z: 8, core: 2. Of those that a mesh axis runs over, the one named last changes fastest.
Arguments:
- features: bfloat16 [32768, 256], P('rows'), may hold values from -6 to 6
- weight: bfloat16 [256, 256], replicated, may hold values from -0.375 to 0.375
- cotangent: bfloat16 [32768, 256], P('rows'), may hold values from -6 to 6
- tile_coords: int32 [128, 4, 20, 2], P('rows', 'rep'), may hold values from 0 to 255, as said below
- tile_count: int32 [128, 4], P('rows', 'rep'), may hold values from 0 to 20, as said below
- tiles: bfloat16 [128, 4, 20, 128, 128], P('rows', 'rep'), as said below
Outputs:
- activation: bfloat16 [32768, 256], P('rows')
- input_grad: bfloat16 [32768, 256], P('rows')
- weight_grad: float32 [256, 256], replicated
Inputs may be any that keep to these rules, and one draw needn't show every extreme that they name: `tile_coords`: entry k of device (i, j)'s list holds a tile row below 2 and a global tile column c with (c // 2) % 4 == j; live entries come first and name distinct tiles; every nonzero tile of A is listed on exactly one device; padding entries hold tile row 0 and a column of the device's first section. `tile_count`: in every draw some device's list is full. `tiles`: A is symmetric: the tile at (r, c) is the transpose of the tile at (c, r); slots at or beyond a device's tile_count hold zeros.
All inputs are finite; a program needn't handle non-finite values.
Results may differ from a plain program's by a relative error of at most 0.006.
Values may be sent and summed in bfloat16 or wider, within the bound.
A program may use at most 64 MiB of HBM per device.

v0:
```python
import math

import jax
import jax.numpy as jnp
from jax import lax
from jax.sharding import PartitionSpec as P


def dsilu(value):
    sigma = jax.nn.sigmoid(value)
    return sigma * (1.0 + value * (1.0 - sigma))


def on_device(features, weight, cotangent, tile_coords, tile_count, tiles):
    rows_total = lax.axis_size("rows")
    rep_total = lax.axis_size("rep")
    rep_me = lax.axis_index("rep")
    tile_rows = tiles.shape[-1]
    width = features.shape[1]
    rows_dev = features.shape[0]
    per_dev = rows_dev // tile_rows
    section_total = rows_total // rep_total
    coords = tile_coords[0, 0]
    live_count = tile_count[0, 0]
    blocks = tiles[0, 0]
    slot_total = blocks.shape[0]
    block_len = max(
        (size_try for size_try in range(1, min(16, slot_total) + 1) if slot_total % size_try == 0)
    )
    column = coords[:, 1]
    panel_slot = column // per_dev // rep_total * per_dev + column % per_dev
    row_inside = coords[:, 0]
    quarter = rows_dev // rep_total

    def collect(local):
        mine = lax.dynamic_slice_in_dim(local, rep_me * quarter, quarter, 0)
        every = lax.all_gather(mine, "rows", axis=0, tiled=True)
        every = every.reshape(section_total, rep_total, quarter, width)
        buffer = lax.all_to_all(every, "rep", split_axis=1, concat_axis=1, tiled=True)
        buffer = buffer.reshape(section_total, rows_dev, width)
        return buffer.reshape(section_total * per_dev, tile_rows, width)

    def aggregate(buffer):

        def one_block(index, total):
            start = index * block_len
            part = lax.dynamic_slice_in_dim(blocks, start, block_len, 0)
            where_from = lax.dynamic_slice_in_dim(panel_slot, start, block_len, 0)
            rows_of = lax.dynamic_slice_in_dim(row_inside, start, block_len, 0)
            panel = jnp.take(buffer, where_from, axis=0)
            product = jnp.einsum("kab,kbf->kaf", part, panel, preferred_element_type=jnp.float32)
            valid = start + jnp.arange(block_len, dtype=jnp.int32) < live_count
            picker = (
                (rows_of[None, :] == jnp.arange(per_dev, dtype=jnp.int32)[:, None]) & valid[None, :]
            ).astype(jnp.float32)
            return total + jnp.einsum(
                "rk,kaf->raf", picker, product, precision=lax.Precision.HIGHEST
            )

        trips = (live_count + block_len - 1) // block_len
        total = lax.fori_loop(
            0, trips, one_block, jnp.zeros((per_dev, tile_rows, width), jnp.float32)
        )
        return total.reshape(rows_dev, width)

    scale = 1.0 / math.sqrt(rows_dev * rows_total)
    transformed = jnp.dot(features, weight, preferred_element_type=jnp.float32).astype(jnp.bfloat16)
    partial_fwd = aggregate(collect(transformed))
    aggregated = lax.psum(partial_fwd, "rep")
    activation = jax.nn.silu(aggregated).astype(jnp.bfloat16)
    slope = (cotangent.astype(jnp.float32) * dsilu(aggregated)).astype(jnp.bfloat16)
    partial_back = aggregate(collect(slope))
    backward = lax.psum(partial_back, "rep")
    back_rounded = backward.astype(jnp.bfloat16)
    input_grad = lax.dot_general(
        back_rounded, weight, (((1,), (1,)), ((), ())), preferred_element_type=jnp.float32
    ).astype(jnp.bfloat16)
    weight_term = lax.dot_general(
        features, back_rounded, (((0,), (0,)), ((), ())), preferred_element_type=jnp.float32
    )
    weight_grad = lax.psum(weight_term, "rows") * scale
    return (activation, input_grad, weight_grad)


def solution(mesh):
    placed = (
        P("rows", None),
        P(),
        P("rows", None),
        P("rows", "rep", None, None),
        P("rows", "rep"),
        P("rows", "rep", None, None, None),
    )
    return jax.shard_map(
        on_device,
        mesh=mesh,
        in_specs=placed,
        out_specs=(P("rows", None), P("rows", None), P()),
        check_vma=False,
    )
```

profile of v0, /device:TPU:1, one launch (start us, length us, event | category | flops | bytes accessed | tf_op | source)
XLA Modules:
  0.0 595.8 jit_solution(16170861087474312081)
XLA Ops:
  7.2 0.0 copy-start
  7.2 0.0 all-gather.3.cloned.1.call-start
  7.2 0.8 copy-done
  8.1 1.1 fusion.43
  9.2 0.6 dynamic-slice_convert_fusion
  9.8 0.0 all-gather.3.cloned.1.call-update
  9.8 92.5 %all-gather.3.cloned.1.call-done = bf16[8192,256]{1,0:T(8,128)(2,1)} async-done(((bf16[64,256]{1,0:T(8,128)(2,1)}), bf16[8192,256]{1,0:T(8,128)(2,1)}) %all-gather.3.cloned.1.call-update) | async-done | bytes 4194320 | tf_op jit(solution)/shard_map/all_gather | solution.py:37
  102.3 4.8 copy.22
  107.1 5.0 all-to-all-start
  112.1 0.0 all-reduce.4.cloned.1.call-start
  112.8 0.0 copy-start.1
  112.8 48.0 %all-to-all-done = bf16[32,4,64,256]{3,2,0,1:T(8,128)(2,1)} async-done(((bf16[32,4,64,256]{3,2,0,1:T(8,128)(2,1)}), bf16[32,4,64,256]{3,2,0,1:T(8,128)(2,1)}, u32[]{:S(2)}, u32[]{:S(2)}) %all-to-all-start) | async-done | bytes 4194336 | tf_op jit(solution)/shard_map/all_to_all | solution.py:39
  160.8 4.8 copy.23
  165.6 0.1 broadcast.62.clone
  165.7 6.1 %while.20 = (s32[]{:T(128)}, f32[2,128,256]{2,0,1:T(2,128)S(1)}, s32[]{:T(128)}, s32[20]{0:T(128)S(1)}, s32[]{:T(128)}, /*index=5*/bf16[20,128,128]{2,1,0:T(8,12...) while((s32[]{:T(128)}, f32[2,128,256]{2,0,1:T(2,128)S(1)}, ...), condition=%wide.region_1.3_spmd, body=%wide.region_0.2_spmd.sunk | while | flops 92144768 | bytes 5444589 | solution.py:61
  165.7 0.7 compare_and_fusion.4
  166.4 2.8 gather_fusion
  169.2 0.4 fusion.66
  169.6 0.1 dynamic_slice.55
  169.7 2.1 fusion.67
  171.8 0.7 copy.24
  172.5 0.0 all-reduce.4.cloned.1.call-update
  172.5 0.0 all-gather.5.cloned.1.call-start
  172.6 48.9 %all-reduce.4.cloned.1.call-done = f32[256,256]{1,0:T(8,128)} async-done(((f32[256,256]{1,0:T(8,128)}), f32[256,256]{1,0:T(8,128)}) %all-reduce.4.cloned.1.call-update) | async-done | bytes 262160 | tf_op jit(solution)/shard_map/psum | solution.py:69
  221.4 1.7 add_divide_fusion
  223.1 1.5 fusion.39
  224.6 0.0 all-gather.5.cloned.1.call-update
  224.6 88.8 %all-gather.5.cloned.1.call-done = bf16[8192,256]{1,0:T(8,128)(2,1)} async-done(((bf16[64,256]{1,0:T(8,128)(2,1)}), bf16[8192,256]{1,0:T(8,128)(2,1)}) %all-gather.5.cloned.1.call-update) | async-done | bytes 4194320 | tf_op jit(solution)/shard_map/all_gather | solution.py:37
  313.4 4.8 copy.25
  318.2 4.8 all-to-all-start.1
  323.0 0.0 all-reduce.6.cloned.1.call-start
  323.1 48.7 %all-to-all-done.1 = bf16[32,4,64,256]{3,2,0,1:T(8,128)(2,1)} async-done(((bf16[32,4,64,256]{3,2,0,1:T(8,128)(2,1)}), bf16[32,4,64,256]{3,2,0,1:T(8,128)(2,1)}, u32[]{:S(2)}, u32[]{:S(2)}) %all-to-all-start.1) | async-done | bytes 4194336 | tf_op jit(solution)/shard_map/all_to_all | solution.py:39
  371.8 4.8 copy.26
  376.5 0.1 broadcast.62
  376.6 0.0 copy-start.2
  376.6 6.1 %while.21 = (s32[]{:T(128)}, f32[2,128,256]{2,0,1:T(2,128)S(1)}, s32[]{:T(128)}, s32[20]{0:T(128)S(1)}, s32[]{:T(128)}, /*index=5*/bf16[20,128,128]{2,1,0:T(8,12...) while((s32[]{:T(128)}, f32[2,128,256]{2,0,1:T(2,128)S(1)}, ...), condition=%wide.region_4.6_spmd, body=%wide.region_3.5_spmd.sunk | while | flops 92144768 | bytes 5444589 | solution.py:61
  376.6 0.8 compare_and_fusion.5
  377.4 2.8 gather_fusion.1
  380.2 0.4 fusion.72
  380.6 0.1 dynamic_slice.57
  380.7 2.1 fusion.73
  382.8 15.1 %all-reduce.7 = bf16[256,256]{1,0:T(8,128)(2,1)S(1)} all-reduce(f32[256,256]{1,0:T(8,128)S(1)} %bitcast.49), channel_id=1, replica_groups=mesh['rows'=128,'rep'=4] {'rep'}, use_global_device_ids=true, to_apply=%region_5.7 | all-reduce | flops 65536 | bytes 393216 | tf_op jit(solution)/shard_map/psum | solution.py:73
  397.9 0.9 convolution_bitcast_fusion
  398.8 0.0 all-reduce.6.cloned.1.call-update
  398.8 0.9 convolution_convert_fusion
  399.7 187.7 %all-reduce.6.cloned.1.call-done = f32[256,256]{0,1:T(8,128)} async-done(((f32[256,256]{0,1:T(8,128)}), f32[256,256]{0,1:T(8,128)}) %all-reduce.6.cloned.1.call-update) | async-done | bytes 262160 | tf_op jit(solution)/shard_map/psum | solution.py:81
  587.4 1.0 broadcast_multiply_fusion
  588.4 0.8 copy.28
  (9 shorter events, 0.1 us)
Async XLA Ops:
  7.2 0.9 copy-start
  7.2 95.2 %all-gather.3.cloned.1.call-start = ((), (), s32[]{:S(2)}) async-start(), calls=%async_computation.2 | async-start | bytes 4227072 | tf_op jit(solution)/shard_map/all_gather | solution.py:37
  107.1 5.7 copy-start.3
  107.1 53.7 %all-to-all-start = ((bf16[32,4,64,256]{3,2,0,1:T(8,128)(2,1)}), bf16[32,4,64,256]{3,2,0,1:T(8,128)(2,1)}, u32[]{:S(2)}, u32[]{:S(2)}) async-start(bf16[32,4,64,256]{3,2,0,1:T(8,128)(2,1)} %copy.22), calls=%async_computation | async-start | bytes 8388608 | tf_op jit(solution)/shard_map/all_to_all | solution.py:39
  112.1 109.4 %all-reduce.4.cloned.1.call-start = ((), (), s32[]{:S(2)}) async-start(), calls=%async_computation.3 | async-start | bytes 524288 | tf_op jit(solution)/shard_map/psum | solution.py:69
  112.8 52.8 %copy-start.1 = (bf16[1,1,20,128,128]{4,3,2,1,0:T(8,128)(2,1)S(1)}, bf16[1,1,20,128,128]{4,3,2,1,0:T(8,128)(2,1)}, u32[]{:S(2)}) copy-start(bf16[1,1,20,128,128]{4,3,2,1,0:T(8,128)(2,1)} %param.17) | copy-start | bytes 1966084
  172.5 140.9 %all-gather.5.cloned.1.call-start = ((), (), s32[]{:S(2)}) async-start(), calls=%async_computation.4 | async-start | bytes 4227072 | tf_op jit(solution)/shard_map/all_gather | solution.py:37
  318.2 53.6 %all-to-all-start.1 = ((bf16[32,4,64,256]{3,2,0,1:T(8,128)(2,1)}), bf16[32,4,64,256]{3,2,0,1:T(8,128)(2,1)}, u32[]{:S(2)}, u32[]{:S(2)}) async-start(bf16[32,4,64,256]{3,2,0,1:T(8,128)(2,1)} %copy.25), calls=%async_computation.1 | async-start | bytes 8388608 | tf_op jit(solution)/shard_map/all_to_all | solution.py:39
  323.0 264.4 %all-reduce.6.cloned.1.call-start = ((), (), s32[]{:S(2)}) async-start(), calls=%async_computation.5 | async-start | bytes 524288 | tf_op jit(solution)/shard_map/psum | solution.py:81
  376.6 22.3 %copy-start.2 = (bf16[256,256]{1,0:T(8,128)(2,1)S(1)}, bf16[256,256]{1,0:T(8,128)(2,1)}, u32[]{:S(2)}) copy-start(bf16[256,256]{1,0:T(8,128)(2,1)} %param.13) | copy-start | bytes 393220
Sparse Core Ops, SparseCore 0:
  11.7 90.5 all-gather.2
  172.6 48.7 all-reduce.3
  225.6 87.7 all-gather.4
  399.0 188.4 all-reduce.5
where the time goes:
time: 597 us; the launch traced here: 596 us
  waiting for transfers between devices  515 us (86%)
  local copies, waits for them, and re-layouts  27.9 us (5%)
  blocking collectives  15.1 us (3%)
  between operations  14.6 us (2%)
  starting transfers between devices  9.98 us (2%)
  matrix products  7.83 us (1%)
    psum x1, waiting for transfers between devices, on_device(): weight_grad = lax.psum(weight_term, 'rows') * scale  188 us
    all_gather x2, waiting for transfers between devices, collect(): every = lax.all_gather(mine, 'rows', axis=0, tiled=True)  181 us
    all_to_all x2, waiting for transfers between devices, collect(): lax.all_to_all(every, 'rep', split_axis=1, concat_axis=1, tiled=True)  96.7 us
    psum x1, waiting for transfers between devices, on_device(): aggregated = lax.psum(partial_fwd, 'rep')  48.9 us
    psum x1, blocking collectives, on_device(): backward = lax.psum(partial_back, 'rep')  15.1 us
  transfers between devices with their start and end apart: 6, of which 6 were waited for; matrix products, arithmetic and copies ran while one was open for 0% of the time, Pallas kernels for 0%

commit v1 on v0

v1 whole, which is shorter than its diff:
```python
import functools
import math

import jax
import jax.numpy as jnp
from jax import lax
from jax.experimental import pallas as pl
from jax.experimental.pallas import tpu as pltpu
from jax.sharding import PartitionSpec as P

MESH = pl.DeviceIdType.MESH
NX, NY, NZ = 4, 8, 8
NS = NY // 2
HALF = NS * NZ
ROWS, F, TILE, KMAX = 256, 256, 128, 20
BF, F32 = jnp.bfloat16, jnp.float32


def at(x, y, z, k):
    return ((z * NY + y) * 2 + k, x)


def start(src, dst, send_sem, recv_sem, device):
    pltpu.make_async_remote_copy(
        src_ref=src, dst_ref=dst, send_sem=send_sem, recv_sem=recv_sem,
        device_id=device, device_id_type=MESH,
    ).start()


def wait(ref, sem):
    pltpu.make_async_copy(ref, ref, sem).wait()


def loop(low, high, body):
    def step(index, carry):
        body(index)
        return carry

    lax.fori_loop(low, high, step, 0)


class Place:
    def __init__(self):
        rows = lax.axis_index("rows")
        self.x = lax.axis_index("rep")
        self.k = rows % 2
        self.y = (rows // 2) % NY
        self.z = rows // (2 * NY)
        self.parity = self.x // 2
        self.owner = self.x % 2
        self.on_row = self.y % 2 == self.parity
        self.source = self.on_row & (self.k == self.owner)
        self.yy = self.y // 2


def z_near(me, o):
    step = jnp.where(o % 2 == 1, (o + 1) // 2, NZ - o // 2)
    return (me.z + step) % NZ


def row_near(me, m):
    on = jnp.where(m == 0, 0, jnp.where(m == 1, 2, jnp.where(m == 2, NY - 2, 4)))
    off = jnp.where(m == 0, NY - 1, jnp.where(m == 1, 1, jnp.where(m == 2, NY - 3, 3)))
    return ((me.y + jnp.where(me.on_row, on, off)) % NY) // 2


def gather_begin(me, pan, recv, sent):
    @pl.when(me.source)
    def _():
        first = me.yy * NZ + me.z
        second = me.z * NS + me.yy

        def along(o):
            start(pan.at[first], pan.at[first], sent, recv.at[first],
                  at(me.x, me.y, z_near(me, o), 0))
            step = jnp.where(o % 2 == 1, (o + 1) // 2, NY - o // 2)
            start(pan.at[HALF + second], pan.at[HALF + second], sent, recv.at[second],
                  at(me.x, (me.y + step) % NY, me.z, 1))

        loop(1, NZ, along)

        @pl.when(me.owner == 1)
        def _():
            start(pan.at[first], pan.at[first], sent, recv.at[first], at(me.x, me.y, me.z, 0))

        @pl.when(me.owner == 0)
        def _():
            start(pan.at[HALF + second], pan.at[HALF + second], sent, recv.at[second],
                  at(me.x, me.y, me.z, 1))


def gather_first(me, pan, recv, sent, pair):
    up = at(me.x, (me.y + 1) % NY, me.z, 0)
    down = at(me.x, (me.y + NY - 1) % NY, me.z, 0)

    def send(slot, device):
        start(pan.at[slot], pan.at[slot], sent, recv.at[slot], device)

    def share(slot):
        start(pan.at[slot], pan.at[slot], sent, pair, at(me.x, me.y, me.z, 1))

    def arrived(slot):
        wait(pan.at[slot], recv.at[slot])

    @pl.when(me.on_row)
    def _():
        def own(o):
            slot = me.yy * NZ + z_near(me, o)

            @pl.when((o > 0) | (me.owner == 1))
            def _():
                arrived(slot)

            send(slot, up)
            send(slot, down)

            @pl.when((o > 0) | (me.owner == 0))
            def _():
                share(slot)

        loop(0, NZ, own)

        def near(o):
            zs = z_near(me, o)
            below = ((me.yy + NS - 1) % NS) * NZ + zs
            arrived(below)
            send(below, up)
            share(below)
            above = ((me.yy + 1) % NS) * NZ + zs
            arrived(above)
            send(above, down)
            share(above)

        loop(0, NZ, near)

        def far(o):
            slot = ((me.yy + 2) % NS) * NZ + z_near(me, o)
            arrived(slot)
            share(slot)

        loop(0, NZ, far)

    @pl.when(jnp.logical_not(me.on_row))
    def _():
        skew = 3

        def step(t):
            @pl.when(t < NZ)
            def _():
                zs = z_near(me, t)
                below = (((me.y + NY - 1) % NY) // 2) * NZ + zs
                arrived(below)
                send(below, up)
                share(below)
                above = (((me.y + 1) % NY) // 2) * NZ + zs
                arrived(above)
                send(above, down)
                share(above)

            @pl.when(t >= skew)
            def _():
                o = t - skew
                zs = z_near(me, o)
                below = (((me.y + NY - 3) % NY) // 2) * NZ + zs
                arrived(below)

                @pl.when(o % 2 == 0)
                def _():
                    send(below, up)

                share(below)
                above = (((me.y + 3) % NY) // 2) * NZ + zs
                arrived(above)

                @pl.when(o % 2 == 1)
                def _():
                    send(above, down)

                share(above)

        loop(0, NZ + skew, step)


def gather_second(me, pan, recv, sent, pair):
    up = at(me.x, me.y, (me.z + 1) % NZ, 1)
    down = at(me.x, me.y, (me.z + NZ - 1) % NZ, 1)

    def send(slot, device):
        start(pan.at[HALF + slot], pan.at[HALF + slot], sent, recv.at[slot], device)

    def share(slot):
        start(pan.at[HALF + slot], pan.at[HALF + slot], sent, pair, at(me.x, me.y, me.z, 0))

    def arrived(slot):
        wait(pan.at[HALF + slot], recv.at[slot])

    def own(m):
        slot = me.z * NS + row_near(me, m)
        mine = me.on_row & (m == 0)

        @pl.when(jnp.logical_not(mine & (me.owner == 1)))
        def _():
            arrived(slot)

        send(slot, up)
        send(slot, down)

        @pl.when(jnp.logical_not(mine & (me.owner == 0)))
        def _():
            share(slot)

    loop(0, NS, own)

    def onward(t):
        distance = 1 + t // NS
        m = t % NS
        row = row_near(me, m)
        below = ((me.z + NZ - distance) % NZ) * NS + row
        arrived(below)

        @pl.when((distance < 3) | (m % 2 == 0))
        def _():
            send(below, up)

        share(below)
        above = ((me.z + distance) % NZ) * NS + row
        arrived(above)

        @pl.when((distance < 3) | (m % 2 == 1))
        def _():
            send(above, down)

        share(above)

    loop(0, 3 * NS, onward)

    def last(m):
        slot = ((me.z + 4) % NZ) * NS + row_near(me, m)
        arrived(slot)
        share(slot)

    loop(0, NS, last)


def gather(me, pan, recv, sent, pair):
    @pl.when(me.k == 0)
    def _():
        gather_first(me, pan, recv, sent, pair)

    @pl.when(me.k == 1)
    def _():
        gather_second(me, pan, recv, sent, pair)

    @pl.when(me.source)
    def _():
        wait(pan.at[pl.ds(0, HALF - 1)], pair)

    @pl.when(jnp.logical_not(me.source))
    def _():
        wait(pan.at[pl.ds(0, HALF)], pair)


def gather_end(me, pan, sent):
    first = jnp.where(me.on_row, 4 * NZ, 3 * NZ)
    second = 7 * NS
    count = jnp.where(me.k == 0, first, second) + HALF
    count = count - jnp.where(me.on_row & (me.k != me.owner), 1, 0)
    count = count + jnp.where(me.source, 2 * (NZ - 1) + 1, 0)
    loop(0, count, lambda i: wait(pan.at[0], sent))


def aggregate(coords, lhs, pan, rhs):
    def pick(i):
        column = coords[0, 0, i, 1]
        section = column // 8
        slot = jnp.where(column % 2 == 0, (section % NS) * NZ + section // NS, HALF + section)
        rhs[pl.ds(pl.multiple_of(i * TILE, TILE), TILE), :] = pan[slot]

    loop(0, KMAX, pick)
    return jnp.dot(lhs[...], rhs[...], preferred_element_type=F32)


def kernel(features, weight, cotangent, coords, tiles, act_ref, grad_ref, wg_ref,
           pan1, pan2, lhs, rhs, hx, slope_ref, wgp, wy, wz, wall, bp, bx, ig,
           recv1, recv2, sent1, sent2, pair1, pair2, hx_recv, hx_sent,
           wy_recv, wz_recv, wq_recv, wx_recv, w_sent, wx_sent, bx_recv, ig_recv, b_sent):
    me = Place()
    x, y, z, k = me.x, me.y, me.z, me.k

    barrier = pltpu.get_barrier_semaphore()

    def hello(d):
        for core in range(2):
            pl.semaphore_signal(barrier, inc=1, device_id=at(x, (y + d) % NY, z, core),
                                device_id_type=MESH)
            pl.semaphore_signal(barrier, inc=1, device_id=at(x, y, (z + d) % NZ, core),
                                device_id_type=MESH)

    loop(1, NY, hello)
    for d in range(1, NX):
        pl.semaphore_signal(barrier, inc=1, device_id=at((x + d) % NX, y, z, k),
                            device_id_type=MESH)
    pl.semaphore_signal(barrier, inc=1, device_id=at(x, y, z, 1 - k), device_id_type=MESH)

    @pl.when(me.source)
    def _():
        pan1[me.yy * NZ + z] = features[0:TILE, :]
        pan1[HALF + z * NS + me.yy] = features[TILE:, :]

    pl.semaphore_wait(barrier, 4 * (NY - 1) + NX)

    gather_begin(me, pan1, recv1, sent1)

    def lay(i):
        row = coords[0, 0, i, 0]
        tile = tiles[0, 0, i]
        columns = pl.ds(pl.multiple_of(i * TILE, TILE), TILE)
        zero = jnp.zeros_like(tile)
        lhs[0:TILE, columns] = jnp.where(row == 0, tile, zero)
        lhs[TILE:, columns] = jnp.where(row == 0, zero, tile)

    loop(0, KMAX, lay)

    gather(me, pan1, recv1, sent1, pair1)
    hx[x] = aggregate(coords, lhs, pan1, rhs).astype(BF)

    home = 2 * (y % 2) + k

    def give(d):
        to = (home + d) % NX

        @pl.when(to != x)
        def _():
            start(hx.at[x], hx.at[x], hx_sent, hx_recv.at[x], at(to, y, z, k))

    loop(0, NX, give)

    def middle():
        def take(d):
            wait(hx.at[(x + d) % NX], hx_recv.at[(x + d) % NX])

        loop(1, NX, take)
        hidden = (hx[0].astype(F32) + hx[1].astype(F32)) + (hx[2].astype(F32) + hx[3].astype(F32))
        hidden = hidden.astype(BF)
        hx[x] = hidden
        v = jnp.dot(hidden, weight[...], preferred_element_type=F32)
        s = 1.0 / (1.0 + jnp.exp(-v))
        slope_ref[...] = (cotangent[...].astype(F32) * (s * (1.0 + v * (1.0 - s)))).astype(BF)
        act_ref[...] = (v * s).astype(BF)

    def hx_done():
        loop(1, NX, lambda d: wait(hx.at[0], hx_sent))

    hx_done()

    @pl.when(me.source)
    def _():
        middle()
        pan2[me.yy * NZ + z] = slope_ref[0:TILE, :]
        pan2[HALF + z * NS + me.yy] = slope_ref[TILE:, :]

    gather_begin(me, pan2, recv2, sent2)
    gather(me, pan2, recv2, sent2, pair2)

    @pl.when(jnp.logical_not(me.source))
    def _():
        middle()

    term = lax.dot_general(hx[x], slope_ref[...], (((0,), (0,)), ((), ())),
                           preferred_element_type=F32)
    wgp[0] = term[:, 0:TILE]
    wgp[1] = term[:, TILE:]
    mine = y * 2 + k

    def chunk(to):
        return wgp.at[to % 2, pl.ds(pl.multiple_of(x * 64 + (to // 2) * 8, 8), 8), :]

    def scatter_y(d):
        to = (mine + d) % 16
        start(chunk(to), wy.at[mine], w_sent, wy_recv.at[mine], at(x, to // 2, z, to % 2))

    loop(1, 16, scatter_y)
    wy[mine] = chunk(mine)[...]

    back = aggregate(coords, lhs, pan2, rhs)
    bp[...] = back.astype(BF).reshape(NX, 64, F)

    def give_back(d):
        to = (x + d) % NX
        start(bp.at[to], bx.at[x], b_sent, bx_recv.at[x], at(to, y, z, k))

    loop(1, NX, give_back)
    bx[x] = bp[x]

    def take_y(d):
        src = (mine + d) % 16
        wait(wy.at[src], wy_recv.at[src])

    loop(1, 16, take_y)
    wz[z] = jnp.sum(wy[...], axis=0)

    def scatter_z(d):
        start(wz.at[z], wz.at[z], w_sent, wz_recv.at[z], at(x, y, (z + d) % NZ, k))

    loop(1, NZ, scatter_z)

    def take_back(d):
        wait(bx.at[(x + d) % NX], bx_recv.at[(x + d) % NX])

    loop(1, NX, take_back)
    total = (bx[0].astype(F32) + bx[1].astype(F32)) + (bx[2].astype(F32) + bx[3].astype(F32))
    ig[x] = lax.dot_general(total.astype(BF), weight[...], (((1,), (1,)), ((), ())),
                            preferred_element_type=F32).astype(BF)

    def give_grad(d):
        start(ig.at[x], ig.at[x], b_sent, ig_recv.at[x], at((x + d) % NX, y, z, k))

    loop(1, NX, give_grad)

    def take_z(d):
        src = (z + d) % NZ
        wait(wz.at[src], wz_recv.at[src])

    loop(1, NZ, take_z)
    wall[x, mine] = jnp.sum(wz[...], axis=0) * (1.0 / math.sqrt(ROWS * NY * NZ * 2))

    def spread_y(d):
        to = (mine + d) % 16
        start(wall.at[x, mine], wall.at[x, mine], w_sent, wq_recv.at[mine],
              at(x, to // 2, z, to % 2))

    loop(1, 16, spread_y)

    def take_grad(d):
        wait(ig.at[(x + d) % NX], ig_recv.at[(x + d) % NX])

    loop(1, NX, take_grad)
    grad_ref[...] = ig[...].reshape(ROWS, F)

    def take_q(d):
        src = (mine + d) % 16
        wait(wall.at[x, src], wq_recv.at[src])

    loop(1, 16, take_q)

    def spread_x(d):
        start(wall.at[x], wall.at[x], wx_sent, wx_recv.at[x], at((x + d) % NX, y, z, k))

    loop(1, NX, spread_x)

    gather_end(me, pan1, sent1)
    gather_end(me, pan2, sent2)
    loop(0, 15 + 7 + 15, lambda i: wait(wz.at[0], w_sent))
    loop(0, 6, lambda i: wait(bp.at[0], b_sent))

    def take_x(d):
        wait(wall.at[(x + d) % NX], wx_recv.at[(x + d) % NX])

    loop(1, NX, take_x)
    loop(1, NX, lambda d: wait(wall.at[0], wx_sent))
    for quarter in range(NX):
        for row in range(8):
            for half in range(2):
                wg_ref[quarter * 64 + row * 8:quarter * 64 + row * 8 + 8,
                       half * TILE:(half + 1) * TILE] = wall[quarter, row * 2 + half]


def on_device(features, weight, cotangent, tile_coords, tile_count, tiles):
    vmem = pl.BlockSpec(memory_space=pltpu.VMEM)
    smem = pl.BlockSpec(memory_space=pltpu.SMEM)
    dma = pltpu.SemaphoreType.DMA
    return pl.pallas_call(
        kernel,
        out_shape=(
            jax.ShapeDtypeStruct((ROWS, F), BF),
            jax.ShapeDtypeStruct((ROWS, F), BF),
            jax.ShapeDtypeStruct((F, F), F32),
        ),
        in_specs=[vmem, vmem, vmem, smem, vmem],
        out_specs=(vmem, vmem, vmem),
        scratch_shapes=[
            pltpu.VMEM((2 * HALF, TILE, F), BF),
            pltpu.VMEM((2 * HALF, TILE, F), BF),
            pltpu.VMEM((2 * TILE, KMAX * TILE), BF),
            pltpu.VMEM((KMAX * TILE, F), BF),
            pltpu.VMEM((NX, ROWS, F), BF),
            pltpu.VMEM((ROWS, F), BF),
            pltpu.VMEM((2, F, TILE), F32),
            pltpu.VMEM((16, 8, TILE), F32),
            pltpu.VMEM((NZ, 8, TILE), F32),
            pltpu.VMEM((NX, 16, 8, TILE), F32),
            pltpu.VMEM((NX, 64, F), BF),
            pltpu.VMEM((NX, 64, F), BF),
            pltpu.VMEM((NX, 64, F), BF),
            dma((HALF,)), dma((HALF,)), dma(()), dma(()), dma(()), dma(()),
            dma((NX,)), dma(()),
            dma((16,)), dma((NZ,)), dma((16,)), dma((NX,)), dma(()), dma(()),
            dma((NX,)), dma((NX,)), dma(()),
        ],
        compiler_params=pltpu.CompilerParams(
            collective_id=0, has_side_effects=True, vmem_limit_bytes=40 << 20
        ),
        name="graph_layer",
    )(features, weight, cotangent, tile_coords, tiles)


def solution(mesh):
    placed = (
        P("rows", None),
        P(),
        P("rows", None),
        P("rows", "rep", None, None),
        P("rows", "rep"),
        P("rows", "rep", None, None, None),
    )
    return jax.shard_map(
        on_device,
        mesh=mesh,
        in_specs=placed,
        out_specs=(P("rows", None), P("rows", None), P()),
        check_vma=False,
    )
```

time: 597 us -> 113 us (0.19)
  waiting for transfers between devices: 515 us -> 0 us
  Pallas kernels: 0 us -> 106 us
  local copies, waits for them, and re-layouts: 27.9 us -> 6.58 us
  blocking collectives: 15.1 us -> 0 us
  between operations: 14.6 us -> 0.64 us
  starting transfers between devices: 9.98 us -> 0 us
  matrix products: 7.83 us -> 0 us
    psum x2 -> x0, waiting for transfers between devices: 237 us -> none  [the longest x1 188 us: on_device(): weight_grad = lax.psum(weight_term, 'rows') * scale]
    all_gather x2 -> x0, waiting for transfers between devices: 181 us -> none  [collect(): every = lax.all_gather(mine, 'rows', axis=0, tiled=True)]
    pallas_call x0 -> x1, Pallas kernels: none -> 106 us  [on_device(): pl.pallas_call(kernel, out_shape=(jax.ShapeDtypeStruct((ROWS, F), BF), ja...]
    all_to_all x2 -> x0, waiting for transfers between devices: 96.7 us -> none  [collect(): lax.all_to_all(every, 'rep', split_axis=1, concat_axis=1, tiled=True)]
    psum x1 -> x0, blocking collectives: 15.1 us -> none  [on_device(): backward = lax.psum(partial_back, 'rep')]
    all_to_all x2 -> x0, starting transfers between devices: 9.82 us -> none  [collect(): lax.all_to_all(every, 'rep', split_axis=1, concat_axis=1, tiled=True)]
    all_to_all x2 -> x0, local copies, waits for them, and re-layouts: 9.51 us -> none  [collect(): lax.all_to_all(every, 'rep', split_axis=1, concat_axis=1, tiled=True)]
    reshape x2 -> x0, local copies, waits for them, and re-layouts: 9.51 us -> none  [collect(): every = every.reshape(section_total, rep_total, quarter, width)]
  transfers between devices with their start and end apart: 6 -> 0, of which waited for: 6 -> 0; matrix products, arithmetic and copies ran while one was open for 0% -> 0% of each run, Pallas kernels for 0% -> 0%
where the time goes in v1:
time: 113 us
  Pallas kernels  106 us (94%)
  local copies, waits for them, and re-layouts  6.58 us (6%)
    pallas_call x1, Pallas kernels, on_device(): pl.pallas_call(kernel, out_shape=(jax.ShapeDtypeStruct((ROWS, F), BF), ja...  106 us
    unnamed x12, local copies, waits for them, and re-layouts  6.58 us

profile of v1, /device:TPU:1, one launch (start us, length us, event | category | flops | bytes accessed | tf_op | source)
XLA Modules:
  0.0 112.8 jit_solution(5001901153456487656)
XLA Ops:
  0.6 0.8 copy.8.coords
  1.4 0.0 copy-start
  1.4 1.1 copy-done
  2.5 0.0 copy-start.1
  2.5 0.9 copy-done.1
  3.4 0.0 copy-start.2
  3.4 0.9 copy-done.2
  4.3 0.0 copy-start.3
  4.3 0.9 copy-done.3
  5.2 105.5 %graph_layer.1 = (bf16[256,256]{1,0:T(8,128)(2,1)S(1)}, bf16[256,256]{1,0:T(8,128)(2,1)S(1)}, f32[256,256]{1,0:T(8,128)S(1)}) custom-call(bf16[256,256]{1,0:T(8,128)(2,1)S(1)} %copy-done.1, bf16[256,256]{1,0:T(8,128)(2,1)S(1)} %copy-done.2, bf16[256,256]{1,0:T(8,128)(2,1)S(1)} %copy-done.3, s32[1,1,20,2]{3,2,1,0:T(8,128)S(1)} %copy.8.coords, ...), custom_call_target="tpu_custom_call" | custom-call | tf_op jit(solution)/shard_map/graph_layer/pallas_call | solution.py:472
  110.8 0.7 copy.12
  111.4 0.7 copy.13
  112.1 0.7 copy.14
Async XLA Ops:
  1.4 1.1 copy-start
  2.5 0.9 copy-start.1
  3.4 0.9 copy-start.2
  4.3 0.9 copy-start.3

commit v2 on v1

v2 whole, which is shorter than its diff:
```python
import math

import jax
import jax.numpy as jnp
from jax import lax
from jax.experimental import pallas as pl
from jax.experimental.pallas import tpu as pltpu
from jax.sharding import PartitionSpec as P

MESH = pl.DeviceIdType.MESH
NX, NY, NZ = 4, 8, 8
NS = NY // 2
HALF = NS * NZ
ROWS, F, TILE, KMAX = 256, 256, 128, 20
BF, F32 = jnp.bfloat16, jnp.float32

PARTS = 1
ROOT = (
    ((0, 3), (0, -3), (0, 2), (0, -2), (0, 1), (0, -1), (0, 4), (1, 0), (-1, 0)),
    ((3, 0), (-3, 0), (2, 0), (-2, 0), (1, 0), (-1, 0), (4, 0), (0, 1), (0, -1)),
)
STEPS = {
    (0, True): (
        (0,0,1,(1,0),(-1,0)), (0,0,-1,(1,0),(-1,0)), (0,0,2,(1,0),(-1,0)), (0,0,-2,(1,0),(-1,0)),
        (0,0,3,(1,0),(-1,0)), (0,0,-3,(1,0),(-1,0)), (0,0,4,(1,0),(-1,0)), (0,2,0,(1,0)), (0,-2,0,(-1,0)),
        (0,2,1,(1,0)), (0,-2,1,(-1,0)), (0,2,-1,(1,0)), (0,2,2,(1,0)), (0,-2,-1,(-1,0)), (0,-2,2,(-1,0)),
        (0,2,-2,(1,0)), (0,2,3,(1,0)), (0,-2,-2,(-1,0)), (0,-2,3,(-1,0)), (0,2,-3,(1,0)), (0,-2,-3,(-1,0)),
        (0,2,4,(1,0)), (0,-2,4,(-1,0)), (0,4,0), (0,4,1), (0,4,-1), (0,4,2), (0,4,-2), (0,4,3), (0,4,-3),
        (0,4,4),
    ),
    (0, False): (
        (0,1,0,(1,0)), (0,-1,0,(-1,0)), (0,1,1,(1,0)), (0,-1,1,(-1,0)), (0,1,-1,(1,0)), (0,1,2,(1,0)),
        (0,1,-2,(1,0)), (0,1,3,(1,0)), (0,-1,-1,(-1,0)), (0,-1,2,(-1,0)), (0,-1,-2,(-1,0)), (0,-1,3,(-1,0)),
        (0,1,-3,(1,0)), (0,-1,-3,(-1,0)), (0,1,4,(1,0)), (0,-1,4,(-1,0)), (0,3,0,(1,0)), (0,-3,0),
        (0,3,1,(1,0)), (0,-3,1), (0,3,-1,(1,0)), (0,3,2,(1,0)), (0,-3,-1), (0,-3,2), (0,3,-2,(1,0)),
        (0,3,3,(1,0)), (0,-3,-2), (0,-3,3), (0,3,-3,(1,0)), (0,-3,-3), (0,3,4,(1,0)), (0,-3,4),
    ),
    (1, True): (
        (1,2,0,(0,1),(0,-1)), (1,-2,0,(0,1),(0,-1)), (1,0,1,(0,1)), (1,0,-1,(0,-1)), (1,4,0,(0,1),(0,-1)),
        (1,2,1,(0,1)), (1,-2,1,(0,1)), (1,2,-1,(0,-1)), (1,-2,-1,(0,-1)), (1,0,2,(0,1)), (1,0,-2,(0,-1)),
        (1,4,1,(0,1)), (1,4,-1,(0,-1)), (1,2,2,(0,1)), (1,-2,2,(0,1)), (1,2,-2,(0,-1)), (1,-2,-2,(0,-1)),
        (1,0,3,(0,1)), (1,0,-3), (1,4,2,(0,1)), (1,4,-2,(0,-1)), (1,2,3,(0,1)), (1,-2,3,(0,1)), (1,2,-3),
        (1,-2,-3), (1,0,4), (1,4,3,(0,1)), (1,4,-3), (1,2,4), (1,-2,4), (1,4,4),
    ),
    (1, False): (
        (1,1,0,(0,1),(0,-1)), (1,-1,0,(0,1),(0,-1)), (1,3,0,(0,1),(0,-1)), (1,-3,0,(0,1),(0,-1)),
        (1,1,1,(0,1)), (1,-1,1,(0,1)), (1,1,-1,(0,-1)), (1,3,1,(0,1)), (1,-1,-1,(0,-1)), (1,3,-1,(0,-1)),
        (1,-3,1,(0,1)), (1,-3,-1,(0,-1)), (1,1,2,(0,1)), (1,-1,2,(0,1)), (1,1,-2,(0,-1)), (1,-1,-2,(0,-1)),
        (1,3,2,(0,1)), (1,-3,2,(0,1)), (1,3,-2,(0,-1)), (1,-3,-2,(0,-1)), (1,1,3,(0,1)), (1,-1,3,(0,1)),
        (1,1,-3), (1,-1,-3), (1,3,3,(0,1)), (1,-3,3,(0,1)), (1,3,-3), (1,-3,-3), (1,1,4), (1,-1,4), (1,3,4),
        (1,-3,4),
    ),
}
PIECE = TILE // PARTS


def at(x, y, z, k):
    return ((z * NY + y) * 2 + k, x)


def start(src, dst, send_sem, recv_sem, device):
    pltpu.make_async_remote_copy(
        src_ref=src, dst_ref=dst, send_sem=send_sem, recv_sem=recv_sem,
        device_id=device, device_id_type=MESH,
    ).start()


def wait(ref, sem):
    pltpu.make_async_copy(ref, ref, sem).wait()


def loop(low, high, body):
    def step(index, carry):
        body(index)
        return carry

    lax.fori_loop(low, high, step, 0)


class Place:
    def __init__(self):
        rows = lax.axis_index("rows")
        self.x = lax.axis_index("rep")
        self.k = rows % 2
        self.y = (rows // 2) % NY
        self.z = rows // (2 * NY)
        self.owner = self.x % 2
        self.on_row = self.y % 2 == self.x // 2
        self.source = self.on_row & (self.k == self.owner)
        self.panel = self.z * NS + self.y // 2


class Gather:
    def __init__(self, me, pan, recv, sent, pair):
        self.me, self.pan, self.recv, self.sent, self.pair = me, pan, recv, sent, pair

    def piece(self, p, panel):
        return self.pan.at[(p % 2) * HALF + panel, pl.ds((p // 2) * PIECE, PIECE)]

    def send(self, p, panel, dy, dz):
        ref = self.piece(p, panel)
        device = at(self.me.x, (self.me.y + dy + NY) % NY, (self.me.z + dz + NZ) % NZ, p % 2)
        start(ref, ref, self.sent, self.recv.at[p * HALF + panel], device)

    def begin(self):
        me, pan = self.me, self.pan

        @pl.when(me.source)
        def _():
            sign = 1 - 2 * (me.z % 2)
            for turn in range(max(len(moves) for moves in ROOT)):
                for p, moves in enumerate(ROOT):
                    if turn < len(moves):
                        dy, dz = moves[turn]
                        self.send(p, me.panel, sign * dy, sign * dz)
            for half in range(2):
                ref = pan.at[half * HALF + me.panel]
                start(ref, ref, self.sent, self.pair, at(me.x, me.y, me.z, 1 - me.k))

    def forward(self, low, high):
        me = self.me
        for (core, on_row), steps in STEPS.items():
            part = steps[round(low * len(steps)):round(high * len(steps))]

            @pl.when((me.k == core) & (me.on_row == on_row))
            def _(part=part):
                for p, dy, dz, *moves in part:
                    sign = 1 - 2 * ((me.z + dz) % 2)
                    z = (me.z - sign * dz + NZ) % NZ
                    y = (me.y - sign * dy + NY) % NY
                    panel = z * NS + y // 2
                    ref = self.piece(p, panel)
                    wait(ref, self.recv.at[p * HALF + panel])
                    for my, mz in moves:
                        self.send(p, panel, sign * my, sign * mz)
                    start(ref, ref, self.sent, self.pair, at(me.x, me.y, me.z, 1 - me.k))

    def finish(self):
        me = self.me

        @pl.when(me.source)
        def _():
            wait(self.pan.at[pl.ds(0, HALF - 1)], self.pair)

        @pl.when(me.on_row & jnp.logical_not(me.source))
        def _():
            wait(self.pan.at[pl.ds(0, HALF + 1)], self.pair)

        @pl.when(jnp.logical_not(me.on_row))
        def _():
            wait(self.pan.at[pl.ds(0, HALF)], self.pair)

    def end(self):
        me = self.me
        count = jnp.where(me.source, sum(len(moves) for moves in ROOT) + 2 * PARTS, 0)
        for (core, on_row), steps in STEPS.items():
            total = sum(len(step) - 2 for step in steps)
            count = count + jnp.where((me.k == core) & (me.on_row == on_row), total, 0)
        loop(0, count, lambda i: wait(self.piece(0, 0), self.sent))


def aggregate(coords, lhs, pan, rhs):
    def pick(i):
        column = coords[0, 0, 1, i]
        slot = (column % 2) * HALF + column // 8
        rhs[pl.ds(pl.multiple_of(i * TILE, TILE), TILE), :] = pan[slot]

    loop(0, KMAX, pick)
    return jnp.dot(lhs[...], rhs[...], preferred_element_type=F32)


def kernel(features, weight_in, cotangent_in, coords, tiles_in, act_ref, grad_ref, wg_ref,
           pan1, pan2, weight, cotangent, tiles, lhs, rhs, hx, hid, slope_ref,
           wgp, wy, wz, wall, bp, bx, ig,
           f_sem, w_sem, c_sem, t_sem, recv1, recv2, sent1, sent2, pair1, pair2, hx_recv, hx_sent,
           wy_recv, wz_recv, wq_recv, wx_recv, w_sent, wx_sent, bx_recv, ig_recv, b_sent):
    me = Place()
    x, y, z, k = me.x, me.y, me.z, me.k

    own = [
        pltpu.make_async_copy(features.at[pl.ds(half * TILE, TILE)],
                              pan1.at[half * HALF + me.panel], f_sem.at[half])
        for half in range(2)
    ]

    @pl.when(me.source)
    def _():
        own[0].start()
        own[1].start()

    tiles_copy = pltpu.make_async_copy(tiles_in.at[0, 0], tiles, t_sem)
    tiles_copy.start()
    weight_copy = pltpu.make_async_copy(weight_in, weight, w_sem)
    weight_copy.start()
    cotangent_copy = pltpu.make_async_copy(cotangent_in, cotangent, c_sem)
    cotangent_copy.start()

    barrier = pltpu.get_barrier_semaphore()

    def hello(d):
        for core in range(2):
            pl.semaphore_signal(barrier, inc=1, device_id=at(x, (y + d) % NY, z, core),
                                device_id_type=MESH)
            pl.semaphore_signal(barrier, inc=1, device_id=at(x, y, (z + d) % NZ, core),
                                device_id_type=MESH)

    loop(1, NY, hello)
    for d in range(1, NX):
        pl.semaphore_signal(barrier, inc=1, device_id=at((x + d) % NX, y, z, k),
                            device_id_type=MESH)
    pl.semaphore_signal(barrier, inc=1, device_id=at(x, y, z, 1 - k), device_id_type=MESH)

    @pl.when(me.source)
    def _():
        own[0].wait()
        own[1].wait()

    pl.semaphore_wait(barrier, 4 * (NY - 1) + NX)

    one = Gather(me, pan1, recv1, sent1, pair1)
    two = Gather(me, pan2, recv2, sent2, pair2)
    one.begin()

    tiles_copy.wait()

    def lay(i):
        row = coords[0, 0, 0, i]
        tile = tiles[i]
        columns = pl.ds(pl.multiple_of(i * TILE, TILE), TILE)
        zero = jnp.zeros_like(tile)
        lhs[0:TILE, columns] = jnp.where(row == 0, tile, zero)
        lhs[TILE:, columns] = jnp.where(row == 0, zero, tile)

    loop(0, KMAX, lay)
    weight_copy.wait()
    cotangent_copy.wait()

    one.forward(0, 1)
    one.finish()
    hx[x] = aggregate(coords, lhs, pan1, rhs).astype(BF)

    home = 2 * (y % 2) + k

    def give(d):
        to = (home + d) % NX

        @pl.when(to != x)
        def _():
            start(hx.at[x], hx.at[x], hx_sent, hx_recv.at[x], at(to, y, z, k))

    loop(0, NX, give)

    def middle():
        def take(d):
            wait(hx.at[(x + d) % NX], hx_recv.at[(x + d) % NX])

        loop(1, NX, take)
        hidden = (hx[0].astype(F32) + hx[1].astype(F32)) + (hx[2].astype(F32) + hx[3].astype(F32))
        hid[...] = hidden.astype(BF)
        v = jnp.dot(hid[...], weight[...], preferred_element_type=F32)
        s = 1.0 / (1.0 + jnp.exp(-v))
        slope_ref[...] = (cotangent[...].astype(F32) * (s * (1.0 + v * (1.0 - s)))).astype(BF)
        act_ref[...] = (v * s).astype(BF)

    @pl.when(me.source)
    def _():
        middle()
        pan2[me.panel] = slope_ref[0:TILE, :]
        pan2[HALF + me.panel] = slope_ref[TILE:, :]

    two.begin()
    two.forward(0, CUTS[0])

    @pl.when(jnp.logical_not(me.source))
    def _():
        middle()

    term = lax.dot_general(hid[...], slope_ref[...], (((0,), (0,)), ((), ())),
                           preferred_element_type=F32)
    wgp[0] = term[:, 0:TILE]
    wgp[1] = term[:, TILE:]
    mine = y * 2 + k

    def chunk(to):
        return wgp.at[to % 2, pl.ds(pl.multiple_of(x * 64 + (to // 2) * 8, 8), 8), :]

    def scatter_y(d):
        to = (mine + d) % 16
        start(chunk(to), wy.at[mine], w_sent, wy_recv.at[mine], at(x, to // 2, z, to % 2))

    loop(1, 16, scatter_y)
    wy[mine] = chunk(mine)[...]

    two.forward(CUTS[0], CUTS[1])

    def take_y(d):
        src = (mine + d) % 16
        wait(wy.at[src], wy_recv.at[src])

    loop(1, 16, take_y)
    wz[z] = jnp.sum(wy[...], axis=0)

    def scatter_z(d):
        start(wz.at[z], wz.at[z], w_sent, wz_recv.at[z], at(x, y, (z + d) % NZ, k))

    loop(1, NZ, scatter_z)

    two.forward(CUTS[1], CUTS[2])

    def take_z(d):
        src = (z + d) % NZ
        wait(wz.at[src], wz_recv.at[src])

    loop(1, NZ, take_z)
    wall[x, mine] = jnp.sum(wz[...], axis=0) * (1.0 / math.sqrt(ROWS * NY * NZ * 2))

    def spread_y(d):
        to = (mine + d) % 16
        start(wall.at[x, mine], wall.at[x, mine], w_sent, wq_recv.at[mine],
              at(x, to // 2, z, to % 2))

    loop(1, 16, spread_y)

    two.forward(CUTS[2], 1)
    two.finish()

    bp[...] = aggregate(coords, lhs, pan2, rhs).astype(BF).reshape(NX, 64, F)

    def give_back(d):
        to = (x + d) % NX
        start(bp.at[to], bx.at[x], b_sent, bx_recv.at[x], at(to, y, z, k))

    loop(1, NX, give_back)
    bx[x] = bp[x]

    def take_q(d):
        src = (mine + d) % 16
        wait(wall.at[x, src], wq_recv.at[src])

    loop(1, 16, take_q)

    def spread_x(d):
        start(wall.at[x], wall.at[x], wx_sent, wx_recv.at[x], at((x + d) % NX, y, z, k))

    loop(1, NX, spread_x)

    def take_back(d):
        wait(bx.at[(x + d) % NX], bx_recv.at[(x + d) % NX])

    loop(1, NX, take_back)
    total = (bx[0].astype(F32) + bx[1].astype(F32)) + (bx[2].astype(F32) + bx[3].astype(F32))
    ig[x] = lax.dot_general(total.astype(BF), weight[...], (((1,), (1,)), ((), ())),
                            preferred_element_type=F32).astype(BF)

    def give_grad(d):
        start(ig.at[x], ig.at[x], b_sent, ig_recv.at[x], at((x + d) % NX, y, z, k))

    loop(1, NX, give_grad)

    one.end()
    two.end()
    loop(1, NX, lambda d: wait(hx.at[0], hx_sent))
    loop(0, 15 + 7 + 15, lambda i: wait(wz.at[0], w_sent))

    def take_x(d):
        wait(wall.at[(x + d) % NX], wx_recv.at[(x + d) % NX])

    loop(1, NX, take_x)
    for quarter in range(NX):
        for row in range(8):
            for half in range(2):
                wg_ref[quarter * 64 + row * 8:quarter * 64 + row * 8 + 8,
                       half * TILE:(half + 1) * TILE] = wall[quarter, row * 2 + half]

    def take_grad(d):
        wait(ig.at[(x + d) % NX], ig_recv.at[(x + d) % NX])

    loop(1, NX, take_grad)
    grad_ref[...] = ig[...].reshape(ROWS, F)
    loop(1, NX, lambda d: wait(wall.at[0], wx_sent))
    loop(0, 6, lambda i: wait(bp.at[0], b_sent))


CUTS = (0.3, 0.55, 0.8)


def on_device(features, weight, cotangent, tile_coords, tile_count, tiles):
    vmem = pl.BlockSpec(memory_space=pltpu.VMEM)
    smem = pl.BlockSpec(memory_space=pltpu.SMEM)
    anywhere = pl.BlockSpec(memory_space=pl.ANY)
    dma = pltpu.SemaphoreType.DMA
    return pl.pallas_call(
        kernel,
        out_shape=(
            jax.ShapeDtypeStruct((ROWS, F), BF),
            jax.ShapeDtypeStruct((ROWS, F), BF),
            jax.ShapeDtypeStruct((F, F), F32),
        ),
        in_specs=[anywhere, anywhere, anywhere, smem, anywhere],
        out_specs=(vmem, vmem, vmem),
        scratch_shapes=[
            pltpu.VMEM((2 * HALF, TILE, F), BF),
            pltpu.VMEM((2 * HALF, TILE, F), BF),
            pltpu.VMEM((F, F), BF),
            pltpu.VMEM((ROWS, F), BF),
            pltpu.VMEM((KMAX, TILE, TILE), BF),
            pltpu.VMEM((2 * TILE, KMAX * TILE), BF),
            pltpu.VMEM((KMAX * TILE, F), BF),
            pltpu.VMEM((NX, ROWS, F), BF),
            pltpu.VMEM((ROWS, F), BF),
            pltpu.VMEM((ROWS, F), BF),
            pltpu.VMEM((2, F, TILE), F32),
            pltpu.VMEM((16, 8, TILE), F32),
            pltpu.VMEM((NZ, 8, TILE), F32),
            pltpu.VMEM((NX, 16, 8, TILE), F32),
            pltpu.VMEM((NX, 64, F), BF),
            pltpu.VMEM((NX, 64, F), BF),
            pltpu.VMEM((NX, 64, F), BF),
            dma((2,)), dma(()), dma(()), dma(()),
            dma((2 * PARTS * HALF,)), dma((2 * PARTS * HALF,)), dma(()), dma(()), dma(()), dma(()),
            dma((NX,)), dma(()),
            dma((16,)), dma((NZ,)), dma((16,)), dma((NX,)), dma(()), dma(()),
            dma((NX,)), dma((NX,)), dma(()),
        ],
        compiler_params=pltpu.CompilerParams(
            collective_id=0, has_side_effects=True, vmem_limit_bytes=60 << 20
        ),
        name="graph_layer",
    )(features, weight, cotangent, jnp.swapaxes(tile_coords, 2, 3), tiles)


def solution(mesh):
    placed = (
        P("rows", None),
        P(),
        P("rows", None),
        P("rows", "rep", None, None),
        P("rows", "rep"),
        P("rows", "rep", None, None, None),
    )
    return jax.shard_map(
        on_device,
        mesh=mesh,
        in_specs=placed,
        out_specs=(P("rows", None), P("rows", None), P()),
        check_vma=False,
    )
```

time: 113 us -> 95.4 us (0.84)
  Pallas kernels: 106 us -> 91.6 us
  local copies, waits for them, and re-layouts: 6.58 us -> 2.98 us
    pallas_call x1, Pallas kernels: 106 us -> 91.6 us  [on_device(): pl.pallas_call(kernel, out_shape=(jax.ShapeDtypeStruct((ROWS, F), BF), ja...]
    unnamed x12 -> x7, local copies, waits for them, and re-layouts: 6.58 us -> 2.98 us
where the time goes in v2:
time: 95.4 us; the launch traced here: 95.3 us
  Pallas kernels  91.6 us (96%)
  local copies, waits for them, and re-layouts  2.98 us (3%)
    pallas_call x1, Pallas kernels, on_device(): pl.pallas_call(kernel, out_shape=(jax.ShapeDtypeStruct((ROWS, F), BF), ja...  91.6 us
    unnamed x7, local copies, waits for them, and re-layouts  2.98 us

profile of v2, /device:TPU:1, one launch (start us, length us, event | category | flops | bytes accessed | tf_op | source)
XLA Modules:
  0.0 95.3 jit_solution(11933908510889791989)
XLA Ops:
  0.6 91.6 %graph_layer.1 = (bf16[256,256]{1,0:T(8,128)(2,1)}, bf16[256,256]{1,0:T(8,128)(2,1)}, f32[256,256]{1,0:T(8,128)}) custom-call(bf16[256,256]{1,0:T(8,128)(2,1)} %features.1, bf16[256,256]{1,0:T(8,128)(2,1)} %weight_in.1, bf16[256,256]{1,0:T(8,128)(2,1)} %cotangent_in.1, s32[1,1,2,20]{3,2,1,0:T(2,128)} %bitcast.1, bf16[1,1,20,128,128]{4,3,2,1,0:T(8,128)(2,1)} %tiles_in.1), custom_call_target="tpu_custom_call" | custom-call | tf_op jit(solution)/shard_map/graph_layer/pallas_call | solution.py:392
  92.3 0.0 copy-start.1
  92.3 0.0 copy-start
  92.3 1.6 %copy.11 = bf16[256,256]{1,0:T(8,128)(2,1)} copy(bf16[256,256]{1,0:T(8,128)(2,1)} %get-tuple-element.6) | data formatting | bytes 262144
  93.9 0.0 copy-done.1
  93.9 0.7 copy.12
  94.6 0.0 copy-done
  94.6 0.7 copy.13
Async XLA Ops:
  92.3 1.6 %copy-start.1 = (bf16[256,256]{1,0:T(8,128)(2,1)S(1)}, bf16[256,256]{1,0:T(8,128)(2,1)}, u32[]{:S(2)}) copy-start(bf16[256,256]{1,0:T(8,128)(2,1)} %get-tuple-element.7) | copy-start | bytes 393220
  92.3 2.3 %copy-start = (f32[256,256]{1,0:T(8,128)S(1)}, f32[256,256]{1,0:T(8,128)}, u32[]{:S(2)}) copy-start(f32[256,256]{1,0:T(8,128)} %get-tuple-element.8) | copy-start | bytes 786436

commit v3 on v2

--- a/solution.py
+++ b/solution.py
@@ -16,39 +16,39 @@
 
 PARTS = 1
 ROOT = (
-    ((0, 3), (0, -3), (0, 2), (0, -2), (0, 1), (0, -1), (0, 4), (1, 0), (-1, 0)),
-    ((3, 0), (-3, 0), (2, 0), (-2, 0), (1, 0), (-1, 0), (4, 0), (0, 1), (0, -1)),
+    ((-1,0), (0,1), (0,-3), (2,0), (1,0),),
+    ((0,1), (3,0), (0,-2), (-1,0), (-2,0), (0,-1), (0,2), (1,0),),
 )
 STEPS = {
     (0, True): (
-        (0,0,1,(1,0),(-1,0)), (0,0,-1,(1,0),(-1,0)), (0,0,2,(1,0),(-1,0)), (0,0,-2,(1,0),(-1,0)),
-        (0,0,3,(1,0),(-1,0)), (0,0,-3,(1,0),(-1,0)), (0,0,4,(1,0),(-1,0)), (0,2,0,(1,0)), (0,-2,0,(-1,0)),
-        (0,2,1,(1,0)), (0,-2,1,(-1,0)), (0,2,-1,(1,0)), (0,2,2,(1,0)), (0,-2,-1,(-1,0)), (0,-2,2,(-1,0)),
-        (0,2,-2,(1,0)), (0,2,3,(1,0)), (0,-2,-2,(-1,0)), (0,-2,3,(-1,0)), (0,2,-3,(1,0)), (0,-2,-3,(-1,0)),
-        (0,2,4,(1,0)), (0,-2,4,(-1,0)), (0,4,0), (0,4,1), (0,4,-1), (0,4,2), (0,4,-2), (0,4,3), (0,4,-3),
-        (0,4,4),
+        (0,0,1,(-2,0),(0,1)), (0,2,0,(0,3),(0,1),(1,0),(0,-1)), (0,0,-3,(1,0),(0,1),(0,-1)), (0,-2,0),
+        (0,-2,1,(-1,0),(0,1)), (0,0,2,(-1,0),(0,1)), (0,2,1,(1,0)), (0,2,3,(0,-1),(1,0),(-1,0)),
+        (0,2,-1,(0,-1)), (0,-2,-1), (0,0,4,(-1,0)), (0,0,-2,(1,0)), (0,0,-1), (0,4,0,(0,-3)), (0,0,3),
+        (0,-2,2,(0,1)), (0,-2,-3), (0,-2,-2), (0,2,2,(-1,0)), (0,2,-3,(0,-1),(1,0)), (0,2,-2), (0,4,1,(0,1)),
+        (0,4,-1), (0,-2,3,(0,1)), (0,4,3), (0,4,-3), (0,2,4), (0,4,2), (0,4,-2), (0,4,4), (0,-2,4),
     ),
     (0, False): (
-        (0,1,0,(1,0)), (0,-1,0,(-1,0)), (0,1,1,(1,0)), (0,-1,1,(-1,0)), (0,1,-1,(1,0)), (0,1,2,(1,0)),
-        (0,1,-2,(1,0)), (0,1,3,(1,0)), (0,-1,-1,(-1,0)), (0,-1,2,(-1,0)), (0,-1,-2,(-1,0)), (0,-1,3,(-1,0)),
-        (0,1,-3,(1,0)), (0,-1,-3,(-1,0)), (0,1,4,(1,0)), (0,-1,4,(-1,0)), (0,3,0,(1,0)), (0,-3,0),
-        (0,3,1,(1,0)), (0,-3,1), (0,3,-1,(1,0)), (0,3,2,(1,0)), (0,-3,-1), (0,-3,2), (0,3,-2,(1,0)),
-        (0,3,3,(1,0)), (0,-3,-2), (0,-3,3), (0,3,-3,(1,0)), (0,-3,-3), (0,3,4,(1,0)), (0,-3,4),
+        (0,-1,0,(-2,0),(0,-1),(0,-3),(0,3),(-1,0),(0,1)), (0,1,0,(0,-1),(0,1)), (0,-1,-1,(0,-1),(-1,0),(1,0)),
+        (0,-1,1), (0,-3,0,(0,3),(0,-1),(-1,0)), (0,-1,3), (0,-1,-3,(-1,0)), (0,3,0,(0,-1)), (0,1,1), (0,1,-1),
+        (0,-1,-2,(-1,0)), (0,1,-3,(0,-1),(1,0)), (0,-3,1,(-1,0)), (0,-3,-1,(0,-1),(-1,0)), (0,-1,2),
+        (0,-3,3,(0,1),(0,-1),(-1,0)), (0,3,-1,(0,-1)), (0,3,1,(0,1)), (0,3,3,(0,1)), (0,1,3), (0,1,4,(3,0)),
+        (0,-1,4), (0,-3,-2,(-1,0)), (0,1,-2), (0,-3,4,(0,1)), (0,-3,2), (0,3,-2), (0,3,2), (0,1,2), (0,3,4),
+        (0,3,-3), (0,-3,-3),
     ),
     (1, True): (
-        (1,2,0,(0,1),(0,-1)), (1,-2,0,(0,1),(0,-1)), (1,0,1,(0,1)), (1,0,-1,(0,-1)), (1,4,0,(0,1),(0,-1)),
-        (1,2,1,(0,1)), (1,-2,1,(0,1)), (1,2,-1,(0,-1)), (1,-2,-1,(0,-1)), (1,0,2,(0,1)), (1,0,-2,(0,-1)),
-        (1,4,1,(0,1)), (1,4,-1,(0,-1)), (1,2,2,(0,1)), (1,-2,2,(0,1)), (1,2,-2,(0,-1)), (1,-2,-2,(0,-1)),
-        (1,0,3,(0,1)), (1,0,-3), (1,4,2,(0,1)), (1,4,-2,(0,-1)), (1,2,3,(0,1)), (1,-2,3,(0,1)), (1,2,-3),
-        (1,-2,-3), (1,0,4), (1,4,3,(0,1)), (1,4,-3), (1,2,4), (1,-2,4), (1,4,4),
+        (1,0,1,(0,2),(1,0),(3,0),(-1,0)), (1,0,-2,(0,-1),(2,0),(-1,0),(1,0)), (1,0,-1,(-1,0),(1,0)),
+        (1,-2,0,(0,1),(0,-2),(0,-1)), (1,0,3,(0,1),(1,0),(-2,0),(-1,0)), (1,0,2),
+        (1,0,-3,(1,0),(-2,0),(-1,0)), (1,4,0,(0,2)), (1,2,0), (1,2,-2,(0,-2),(0,-1)), (1,2,1,(0,1)),
+        (1,-2,1,(-1,0)), (1,-2,-2), (1,-2,-1), (1,2,-1), (1,0,4,(-3,0),(1,0)), (1,4,1,(0,2)),
+        (1,-2,3,(-1,0),(0,1)), (1,-2,-3,(-1,0)), (1,4,2), (1,2,-3), (1,-2,2), (1,2,4,(1,0)), (1,2,2,(1,0)),
+        (1,2,3,(1,0)), (1,4,-2,(0,1)), (1,-2,4), (1,4,3), (1,4,-3), (1,4,-1), (1,4,4),
     ),
     (1, False): (
-        (1,1,0,(0,1),(0,-1)), (1,-1,0,(0,1),(0,-1)), (1,3,0,(0,1),(0,-1)), (1,-3,0,(0,1),(0,-1)),
-        (1,1,1,(0,1)), (1,-1,1,(0,1)), (1,1,-1,(0,-1)), (1,3,1,(0,1)), (1,-1,-1,(0,-1)), (1,3,-1,(0,-1)),
-        (1,-3,1,(0,1)), (1,-3,-1,(0,-1)), (1,1,2,(0,1)), (1,-1,2,(0,1)), (1,1,-2,(0,-1)), (1,-1,-2,(0,-1)),
-        (1,3,2,(0,1)), (1,-3,2,(0,1)), (1,3,-2,(0,-1)), (1,-3,-2,(0,-1)), (1,1,3,(0,1)), (1,-1,3,(0,1)),
-        (1,1,-3), (1,-1,-3), (1,3,3,(0,1)), (1,-3,3,(0,1)), (1,3,-3), (1,-3,-3), (1,1,4), (1,-1,4), (1,3,4),
-        (1,-3,4),
+        (1,-1,0,(-2,0)), (1,3,0,(0,-1),(1,0),(-1,0)), (1,1,0), (1,1,1,(1,0),(0,1)), (1,-1,1,(0,1)),
+        (1,3,-1,(0,-1),(-1,0)), (1,3,1,(1,0)), (1,-1,-2,(0,-2)), (1,-3,0,(0,-1),(0,2)), (1,1,-2), (1,1,2),
+        (1,-1,-1), (1,-1,2,(-1,0)), (1,1,-1), (1,1,3,(1,0)), (1,3,-2,(1,0),(0,-1)), (1,-1,3), (1,1,-3,(3,0)),
+        (1,-1,-3), (1,-1,4), (1,-3,-1,(0,-1)), (1,-3,2), (1,-3,1), (1,3,-3), (1,1,4), (1,-3,4,(-1,0)),
+        (1,-3,3), (1,-3,-3), (1,-3,-2), (1,3,2), (1,3,3), (1,3,4),
     ),
 }
 PIECE = TILE // PARTS
@@ -156,7 +156,9 @@
         for (core, on_row), steps in STEPS.items():
             total = sum(len(step) - 2 for step in steps)
             count = count + jnp.where((me.k == core) & (me.on_row == on_row), total, 0)
-        loop(0, count, lambda i: wait(self.piece(0, 0), self.sent))
+        bulk = HALF * PARTS
+        loop(0, count // bulk, lambda i: wait(self.pan.at[pl.ds(0, HALF)], self.sent))
+        loop(0, count % bulk, lambda i: wait(self.piece(0, 0), self.sent))
 
 
 def aggregate(coords, lhs, pan, rhs):
@@ -169,10 +171,10 @@
     return jnp.dot(lhs[...], rhs[...], preferred_element_type=F32)
 
 
-def kernel(features, weight_in, cotangent_in, coords, tiles_in, act_ref, grad_ref, wg_ref,
-           pan1, pan2, weight, cotangent, tiles, lhs, rhs, hx, hid, slope_ref,
+def kernel(features, weight_in, cotangent_in, coords_in, tiles_in, act_ref, grad_ref, wg_ref,
+           coords, pan1, pan2, weight, cotangent, tiles, lhs, rhs, hx, hid, slope_ref,
            wgp, wy, wz, wall, bp, bx, ig,
-           f_sem, w_sem, c_sem, t_sem, recv1, recv2, sent1, sent2, pair1, pair2, hx_recv, hx_sent,
+           f_sem, w_sem, c_sem, t_sem, i_sem, recv1, recv2, sent1, sent2, pair1, pair2, hx_recv, hx_sent, hid_recv,
            wy_recv, wz_recv, wq_recv, wx_recv, w_sent, wx_sent, bx_recv, ig_recv, b_sent):
     me = Place()
     x, y, z, k = me.x, me.y, me.z, me.k
@@ -188,6 +190,8 @@
         own[0].start()
         own[1].start()
 
+    coords_copy = pltpu.make_async_copy(coords_in, coords, i_sem)
+    coords_copy.start()
     tiles_copy = pltpu.make_async_copy(tiles_in.at[0, 0], tiles, t_sem)
     tiles_copy.start()
     weight_copy = pltpu.make_async_copy(weight_in, weight, w_sem)
@@ -221,6 +225,7 @@
     two = Gather(me, pan2, recv2, sent2, pair2)
     one.begin()
 
+    coords_copy.wait()
     tiles_copy.wait()
 
     def lay(i):
@@ -241,22 +246,11 @@
 
     home = 2 * (y % 2) + k
 
-    def give(d):
-        to = (home + d) % NX
-
-        @pl.when(to != x)
-        def _():
-            start(hx.at[x], hx.at[x], hx_sent, hx_recv.at[x], at(to, y, z, k))
-
-    loop(0, NX, give)
+    @pl.when(home != x)
+    def _():
+        start(hx.at[x], hx.at[x], hx_sent, hx_recv.at[x], at(home, y, z, k))
 
     def middle():
-        def take(d):
-            wait(hx.at[(x + d) % NX], hx_recv.at[(x + d) % NX])
-
-        loop(1, NX, take)
-        hidden = (hx[0].astype(F32) + hx[1].astype(F32)) + (hx[2].astype(F32) + hx[3].astype(F32))
-        hid[...] = hidden.astype(BF)
         v = jnp.dot(hid[...], weight[...], preferred_element_type=F32)
         s = 1.0 / (1.0 + jnp.exp(-v))
         slope_ref[...] = (cotangent[...].astype(F32) * (s * (1.0 + v * (1.0 - s)))).astype(BF)
@@ -264,15 +258,30 @@
 
     @pl.when(me.source)
     def _():
+        def take(d):
+            wait(hx.at[(x + d) % NX], hx_recv.at[(x + d) % NX])
+
+        loop(1, NX, take)
+        hidden = (hx[0].astype(F32) + hx[1].astype(F32)) + (hx[2].astype(F32) + hx[3].astype(F32))
+        hid[...] = hidden.astype(BF)
         middle()
         pan2[me.panel] = slope_ref[0:TILE, :]
         pan2[HALF + me.panel] = slope_ref[TILE:, :]
 
     two.begin()
+
+    @pl.when(me.source)
+    def _():
+        def tell(d):
+            start(hid, hid, hx_sent, hid_recv, at((x + d) % NX, y, z, k))
+
+        loop(1, NX, tell)
+
     two.forward(0, CUTS[0])
 
     @pl.when(jnp.logical_not(me.source))
     def _():
+        wait(hid, hid_recv)
         middle()
 
     term = lax.dot_general(hid[...], slope_ref[...], (((0,), (0,)), ((), ())),
@@ -359,7 +368,7 @@
 
     one.end()
     two.end()
-    loop(1, NX, lambda d: wait(hx.at[0], hx_sent))
+    loop(0, jnp.where(me.source, NX - 1, 1), lambda d: wait(hx.at[0], hx_sent))
     loop(0, 15 + 7 + 15, lambda i: wait(wz.at[0], w_sent))
 
     def take_x(d):
@@ -384,21 +393,37 @@
 CUTS = (0.3, 0.55, 0.8)
 
 
+def write_out(act, grad, wg, act_out, grad_out, wg_out, sems):
+    copies = [
+        pltpu.make_async_copy(src, dst, sems.at[i])
+        for i, (src, dst) in enumerate(((act, act_out), (grad, grad_out), (wg, wg_out)))
+    ]
+    for copy in copies:
+        copy.start()
+    for copy in copies:
+        copy.wait()
+
+
+def pin(value):
+    return pltpu.with_memory_space_constraint(value, pltpu.HBM)
+
+
 def on_device(features, weight, cotangent, tile_coords, tile_count, tiles):
     vmem = pl.BlockSpec(memory_space=pltpu.VMEM)
-    smem = pl.BlockSpec(memory_space=pltpu.SMEM)
-    anywhere = pl.BlockSpec(memory_space=pl.ANY)
+    hbm = pl.BlockSpec(memory_space=pltpu.HBM)
     dma = pltpu.SemaphoreType.DMA
-    return pl.pallas_call(
+    shapes = (
+        jax.ShapeDtypeStruct((ROWS, F), BF),
+        jax.ShapeDtypeStruct((ROWS, F), BF),
+        jax.ShapeDtypeStruct((F, F), F32),
+    )
+    results = pl.pallas_call(
         kernel,
-        out_shape=(
-            jax.ShapeDtypeStruct((ROWS, F), BF),
-            jax.ShapeDtypeStruct((ROWS, F), BF),
-            jax.ShapeDtypeStruct((F, F), F32),
-        ),
-        in_specs=[anywhere, anywhere, anywhere, smem, anywhere],
+        out_shape=(pltpu.VMEM((ROWS, F), BF), pltpu.VMEM((ROWS, F), BF), pltpu.VMEM((F, F), F32)),
+        in_specs=[hbm, hbm, hbm, hbm, hbm],
         out_specs=(vmem, vmem, vmem),
         scratch_shapes=[
+            pltpu.SMEM((1, 1, 2, KMAX), jnp.int32),
             pltpu.VMEM((2 * HALF, TILE, F), BF),
             pltpu.VMEM((2 * HALF, TILE, F), BF),
             pltpu.VMEM((F, F), BF),
@@ -416,17 +441,26 @@
             pltpu.VMEM((NX, 64, F), BF),
             pltpu.VMEM((NX, 64, F), BF),
             pltpu.VMEM((NX, 64, F), BF),
-            dma((2,)), dma(()), dma(()), dma(()),
+            dma((2,)), dma(()), dma(()), dma(()), dma(()),
             dma((2 * PARTS * HALF,)), dma((2 * PARTS * HALF,)), dma(()), dma(()), dma(()), dma(()),
-            dma((NX,)), dma(()),
+            dma((NX,)), dma(()), dma(()),
             dma((16,)), dma((NZ,)), dma((16,)), dma((NX,)), dma(()), dma(()),
             dma((NX,)), dma((NX,)), dma(()),
         ],
         compiler_params=pltpu.CompilerParams(
-            collective_id=0, has_side_effects=True, vmem_limit_bytes=60 << 20
+            collective_id=0, has_side_effects=True, vmem_limit_bytes=24 << 20
         ),
         name="graph_layer",
-    )(features, weight, cotangent, jnp.swapaxes(tile_coords, 2, 3), tiles)
+    )(pin(features), pin(weight), pin(cotangent), pin(jnp.swapaxes(tile_coords, 2, 3)), pin(tiles))
+    return pl.pallas_call(
+        write_out,
+        out_shape=shapes,
+        in_specs=[vmem, vmem, vmem],
+        out_specs=(hbm, hbm, hbm),
+        scratch_shapes=[dma((3,))],
+        compiler_params=pltpu.CompilerParams(vmem_limit_bytes=4 << 20),
+        name="write_out",
+    )(*[pltpu.with_memory_space_constraint(result, pltpu.VMEM) for result in results])
 
 
 def solution(mesh):

time: 95.4 us -> 83.3 us (0.87)
  Pallas kernels: 91.6 us -> 81.9 us
  local copies, waits for them, and re-layouts: 2.98 us -> 0 us
    pallas_call x1 -> x2, Pallas kernels: 91.6 us -> 81.9 us  [the longest x1 81.1 us: on_device(): pl.pallas_call(kernel, out_shape=(pltpu.VMEM((ROWS, F), BF), pltpu.VMEM((...]
    unnamed x7 -> x0, local copies, waits for them, and re-layouts: 2.98 us -> none
where the time goes in v3:
time: 83.3 us; the launch traced here: 82.5 us
  Pallas kernels  81.9 us (98%)
    pallas_call x1, Pallas kernels, on_device(): pl.pallas_call(kernel, out_shape=(pltpu.VMEM((ROWS, F), BF), pltpu.VMEM((...  81.1 us

profile of v3, /device:TPU:1, one launch (start us, length us, event | category | flops | bytes accessed | tf_op | source)
XLA Modules:
  0.0 82.5 jit_solution(7839813457806069934)
XLA Ops:
  0.6 81.1 %graph_layer.1 = (bf16[256,256]{1,0:T(8,128)(2,1)S(1)}, bf16[256,256]{1,0:T(8,128)(2,1)S(1)}, f32[256,256]{1,0:T(8,128)S(1)}) custom-call(bf16[256,256]{1,0:T(8,128)(2,1)} %features.1, bf16[256,256]{1,0:T(8,128)(2,1)} %weight_in.1, bf16[256,256]{1,0:T(8,128)(2,1)} %cotangent_in.1, s32[1,1,2,20]{3,2,1,0:T(2,128)} %bitcast.1, ...), custom_call_target="tpu_custom_call" | custom-call | tf_op jit(solution)/shard_map/graph_layer/pallas_call | solution.py:420
  81.7 0.8 write_out.1

commit v4 on v3

--- a/solution.py
+++ b/solution.py
@@ -16,39 +16,45 @@
 
 PARTS = 1
 ROOT = (
-    ((-1,0), (0,1), (0,-3), (2,0), (1,0),),
-    ((0,1), (3,0), (0,-2), (-1,0), (-2,0), (0,-1), (0,2), (1,0),),
+    ((-1,0,1), (0,1,1), (0,-3,1), (2,0,1), (1,0,1),),
+    ((0,1,1), (3,0,1), (0,-2,1), (-1,0,1), (-2,0,1), (0,-1,1), (0,2,1), (1,0,1),),
 )
 STEPS = {
     (0, True): (
-        (0,0,1,(-2,0),(0,1)), (0,2,0,(0,3),(0,1),(1,0),(0,-1)), (0,0,-3,(1,0),(0,1),(0,-1)), (0,-2,0),
-        (0,-2,1,(-1,0),(0,1)), (0,0,2,(-1,0),(0,1)), (0,2,1,(1,0)), (0,2,3,(0,-1),(1,0),(-1,0)),
-        (0,2,-1,(0,-1)), (0,-2,-1), (0,0,4,(-1,0)), (0,0,-2,(1,0)), (0,0,-1), (0,4,0,(0,-3)), (0,0,3),
-        (0,-2,2,(0,1)), (0,-2,-3), (0,-2,-2), (0,2,2,(-1,0)), (0,2,-3,(0,-1),(1,0)), (0,2,-2), (0,4,1,(0,1)),
-        (0,4,-1), (0,-2,3,(0,1)), (0,4,3), (0,4,-3), (0,2,4), (0,4,2), (0,4,-2), (0,4,4), (0,-2,4),
+        (0,0,1,1,(-2,0,1),(0,1,1)), (0,2,0,1,(0,3,1),(0,1,1),(1,0,1),(0,-1,1)),
+        (0,0,-3,1,(1,0,1),(0,1,1),(0,-1,1)), (0,-2,0,1), (0,-2,1,1,(-1,0,1),(0,1,1)),
+        (0,0,2,1,(-1,0,1),(0,1,1)), (0,2,1,1,(1,0,1)), (0,2,3,1,(0,-1,1),(1,0,1),(-1,0,1)),
+        (0,2,-1,1,(0,-1,1)), (0,-2,-1,1), (0,0,4,1,(-1,0,1)), (0,0,-2,1,(1,0,1)), (0,0,-1,1),
+        (0,4,0,1,(0,-3,1)), (0,0,3,1), (0,-2,2,1,(0,1,1)), (0,-2,-3,1), (0,-2,-2,1), (0,2,2,1,(-1,0,1)),
+        (0,2,-3,1,(0,-1,1),(1,0,1)), (0,2,-2,1), (0,4,1,1,(0,1,1)), (0,4,-1,1), (0,-2,3,1,(0,1,1)), (0,4,3,1),
+        (0,4,-3,1), (0,2,4,1), (0,4,2,1), (0,4,-2,1), (0,4,4,1), (0,-2,4,1),
     ),
     (0, False): (
-        (0,-1,0,(-2,0),(0,-1),(0,-3),(0,3),(-1,0),(0,1)), (0,1,0,(0,-1),(0,1)), (0,-1,-1,(0,-1),(-1,0),(1,0)),
-        (0,-1,1), (0,-3,0,(0,3),(0,-1),(-1,0)), (0,-1,3), (0,-1,-3,(-1,0)), (0,3,0,(0,-1)), (0,1,1), (0,1,-1),
-        (0,-1,-2,(-1,0)), (0,1,-3,(0,-1),(1,0)), (0,-3,1,(-1,0)), (0,-3,-1,(0,-1),(-1,0)), (0,-1,2),
-        (0,-3,3,(0,1),(0,-1),(-1,0)), (0,3,-1,(0,-1)), (0,3,1,(0,1)), (0,3,3,(0,1)), (0,1,3), (0,1,4,(3,0)),
-        (0,-1,4), (0,-3,-2,(-1,0)), (0,1,-2), (0,-3,4,(0,1)), (0,-3,2), (0,3,-2), (0,3,2), (0,1,2), (0,3,4),
-        (0,3,-3), (0,-3,-3),
+        (0,-1,0,1,(-2,0,1),(0,-1,1),(0,-3,1),(0,3,1),(-1,0,1),(0,1,1)), (0,1,0,1,(0,-1,1),(0,1,1)),
+        (0,-1,-1,1,(0,-1,1),(-1,0,1),(1,0,1)), (0,-1,1,1), (0,-3,0,1,(0,3,1),(0,-1,1),(-1,0,1)), (0,-1,3,1),
+        (0,-1,-3,1,(-1,0,1)), (0,3,0,1,(0,-1,1)), (0,1,1,1), (0,1,-1,1), (0,-1,-2,1,(-1,0,1)),
+        (0,1,-3,1,(0,-1,1),(1,0,1)), (0,-3,1,1,(-1,0,1)), (0,-3,-1,1,(0,-1,1),(-1,0,1)), (0,-1,2,1),
+        (0,-3,3,1,(0,1,1),(0,-1,1),(-1,0,1)), (0,3,-1,1,(0,-1,1)), (0,3,1,1,(0,1,1)), (0,3,3,1,(0,1,1)),
+        (0,1,3,1), (0,1,4,1,(3,0,1)), (0,-1,4,1), (0,-3,-2,1,(-1,0,1)), (0,1,-2,1), (0,-3,4,1,(0,1,1)),
+        (0,-3,2,1), (0,3,-2,1), (0,3,2,1), (0,1,2,1), (0,3,4,1), (0,3,-3,1), (0,-3,-3,1),
     ),
     (1, True): (
-        (1,0,1,(0,2),(1,0),(3,0),(-1,0)), (1,0,-2,(0,-1),(2,0),(-1,0),(1,0)), (1,0,-1,(-1,0),(1,0)),
-        (1,-2,0,(0,1),(0,-2),(0,-1)), (1,0,3,(0,1),(1,0),(-2,0),(-1,0)), (1,0,2),
-        (1,0,-3,(1,0),(-2,0),(-1,0)), (1,4,0,(0,2)), (1,2,0), (1,2,-2,(0,-2),(0,-1)), (1,2,1,(0,1)),
-        (1,-2,1,(-1,0)), (1,-2,-2), (1,-2,-1), (1,2,-1), (1,0,4,(-3,0),(1,0)), (1,4,1,(0,2)),
-        (1,-2,3,(-1,0),(0,1)), (1,-2,-3,(-1,0)), (1,4,2), (1,2,-3), (1,-2,2), (1,2,4,(1,0)), (1,2,2,(1,0)),
-        (1,2,3,(1,0)), (1,4,-2,(0,1)), (1,-2,4), (1,4,3), (1,4,-3), (1,4,-1), (1,4,4),
+        (1,0,1,1,(0,2,1),(1,0,1),(3,0,1),(-1,0,1)), (1,0,-2,1,(0,-1,1),(2,0,1),(-1,0,1),(1,0,1)),
+        (1,0,-1,1,(-1,0,1),(1,0,1)), (1,-2,0,1,(0,1,1),(0,-2,1),(0,-1,1)),
+        (1,0,3,1,(0,1,1),(1,0,1),(-2,0,1),(-1,0,1)), (1,0,2,1), (1,0,-3,1,(1,0,1),(-2,0,1),(-1,0,1)),
+        (1,4,0,1,(0,2,1)), (1,2,0,1), (1,2,-2,1,(0,-2,1),(0,-1,1)), (1,2,1,1,(0,1,1)), (1,-2,1,1,(-1,0,1)),
+        (1,-2,-2,1), (1,-2,-1,1), (1,2,-1,1), (1,0,4,1,(-3,0,1),(1,0,1)), (1,4,1,1,(0,2,1)),
+        (1,-2,3,1,(-1,0,1),(0,1,1)), (1,-2,-3,1,(-1,0,1)), (1,4,2,1), (1,2,-3,1), (1,-2,2,1),
+        (1,2,4,1,(1,0,1)), (1,2,2,1,(1,0,1)), (1,2,3,1,(1,0,1)), (1,4,-2,1,(0,1,1)), (1,-2,4,1), (1,4,3,1),
+        (1,4,-3,1), (1,4,-1,1), (1,4,4,1),
     ),
     (1, False): (
-        (1,-1,0,(-2,0)), (1,3,0,(0,-1),(1,0),(-1,0)), (1,1,0), (1,1,1,(1,0),(0,1)), (1,-1,1,(0,1)),
-        (1,3,-1,(0,-1),(-1,0)), (1,3,1,(1,0)), (1,-1,-2,(0,-2)), (1,-3,0,(0,-1),(0,2)), (1,1,-2), (1,1,2),
-        (1,-1,-1), (1,-1,2,(-1,0)), (1,1,-1), (1,1,3,(1,0)), (1,3,-2,(1,0),(0,-1)), (1,-1,3), (1,1,-3,(3,0)),
-        (1,-1,-3), (1,-1,4), (1,-3,-1,(0,-1)), (1,-3,2), (1,-3,1), (1,3,-3), (1,1,4), (1,-3,4,(-1,0)),
-        (1,-3,3), (1,-3,-3), (1,-3,-2), (1,3,2), (1,3,3), (1,3,4),
+        (1,-1,0,1,(-2,0,1)), (1,3,0,1,(0,-1,1),(1,0,1),(-1,0,1)), (1,1,0,1), (1,1,1,1,(1,0,1),(0,1,1)),
+        (1,-1,1,1,(0,1,1)), (1,3,-1,1,(0,-1,1),(-1,0,1)), (1,3,1,1,(1,0,1)), (1,-1,-2,1,(0,-2,1)),
+        (1,-3,0,1,(0,-1,1),(0,2,1)), (1,1,-2,1), (1,1,2,1), (1,-1,-1,1), (1,-1,2,1,(-1,0,1)), (1,1,-1,1),
+        (1,1,3,1,(1,0,1)), (1,3,-2,1,(1,0,1),(0,-1,1)), (1,-1,3,1), (1,1,-3,1,(3,0,1)), (1,-1,-3,1),
+        (1,-1,4,1), (1,-3,-1,1,(0,-1,1)), (1,-3,2,1), (1,-3,1,1), (1,3,-3,1), (1,1,4,1), (1,-3,4,1,(-1,0,1)),
+        (1,-3,3,1), (1,-3,-3,1), (1,-3,-2,1), (1,3,2,1), (1,3,3,1), (1,3,4,1),
     ),
 }
 PIECE = TILE // PARTS
@@ -97,25 +103,27 @@
     def piece(self, p, panel):
         return self.pan.at[(p % 2) * HALF + panel, pl.ds((p // 2) * PIECE, PIECE)]
 
-    def send(self, p, panel, dy, dz):
+    def send(self, p, panel, sign, move):
+        dy, dz, cores = move
         ref = self.piece(p, panel)
-        device = at(self.me.x, (self.me.y + dy + NY) % NY, (self.me.z + dz + NZ) % NZ, p % 2)
-        start(ref, ref, self.sent, self.recv.at[p * HALF + panel], device)
-
-    def begin(self):
-        me, pan = self.me, self.pan
-
-        @pl.when(me.source)
-        def _():
-            sign = 1 - 2 * (me.z % 2)
-            for turn in range(max(len(moves) for moves in ROOT)):
-                for p, moves in enumerate(ROOT):
-                    if turn < len(moves):
-                        dy, dz = moves[turn]
-                        self.send(p, me.panel, sign * dy, sign * dz)
-            for half in range(2):
-                ref = pan.at[half * HALF + me.panel]
-                start(ref, ref, self.sent, self.pair, at(me.x, me.y, me.z, 1 - me.k))
+        y = (self.me.y + sign * dy + NY) % NY
+        z = (self.me.z + sign * dz + NZ) % NZ
+        start(ref, ref, self.sent, self.recv.at[p * HALF + panel], at(self.me.x, y, z, p % 2))
+        if cores == 2:
+            start(ref, ref, self.sent, self.pair, at(self.me.x, y, z, 1 - p % 2))
+
+    def root(self, pieces):
+        sign = 1 - 2 * (self.me.z % 2)
+        for turn in range(max(len(ROOT[p]) for p in pieces)):
+            for p in pieces:
+                if turn < len(ROOT[p]):
+                    self.send(p, self.me.panel, sign, ROOT[p][turn])
+
+    def mate(self):
+        me = self.me
+        for half in range(2):
+            ref = self.pan.at[half * HALF + me.panel]
+            start(ref, ref, self.sent, self.pair, at(me.x, me.y, me.z, 1 - me.k))
 
     def forward(self, low, high):
         me = self.me
@@ -124,16 +132,17 @@
 
             @pl.when((me.k == core) & (me.on_row == on_row))
             def _(part=part):
-                for p, dy, dz, *moves in part:
+                for p, dy, dz, share, *moves in part:
                     sign = 1 - 2 * ((me.z + dz) % 2)
                     z = (me.z - sign * dz + NZ) % NZ
                     y = (me.y - sign * dy + NY) % NY
                     panel = z * NS + y // 2
                     ref = self.piece(p, panel)
                     wait(ref, self.recv.at[p * HALF + panel])
-                    for my, mz in moves:
-                        self.send(p, panel, sign * my, sign * mz)
-                    start(ref, ref, self.sent, self.pair, at(me.x, me.y, me.z, 1 - me.k))
+                    for move in moves:
+                        self.send(p, panel, sign, move)
+                    if share:
+                        start(ref, ref, self.sent, self.pair, at(me.x, me.y, me.z, 1 - me.k))
 
     def finish(self):
         me = self.me
@@ -152,9 +161,9 @@
 
     def end(self):
         me = self.me
-        count = jnp.where(me.source, sum(len(moves) for moves in ROOT) + 2 * PARTS, 0)
+        count = jnp.where(me.source, sum(move[2] for moves in ROOT for move in moves) + 2 * PARTS, 0)
         for (core, on_row), steps in STEPS.items():
-            total = sum(len(step) - 2 for step in steps)
+            total = sum(step[3] + sum(move[2] for move in step[4:]) for step in steps)
             count = count + jnp.where((me.k == core) & (me.on_row == on_row), total, 0)
         bulk = HALF * PARTS
         loop(0, count // bulk, lambda i: wait(self.pan.at[pl.ds(0, HALF)], self.sent))
@@ -223,7 +232,11 @@
 
     one = Gather(me, pan1, recv1, sent1, pair1)
     two = Gather(me, pan2, recv2, sent2, pair2)
-    one.begin()
+
+    @pl.when(me.source)
+    def _():
+        one.root(range(2 * PARTS))
+        one.mate()
 
     coords_copy.wait()
     tiles_copy.wait()
@@ -242,36 +255,40 @@
 
     one.forward(0, 1)
     one.finish()
-    hx[x] = aggregate(coords, lhs, pan1, rhs).astype(BF)
+    partial = aggregate(coords, lhs, pan1, rhs)
 
     home = 2 * (y % 2) + k
-
-    @pl.when(home != x)
-    def _():
-        start(hx.at[x], hx.at[x], hx_sent, hx_recv.at[x], at(home, y, z, k))
-
-    def middle():
-        v = jnp.dot(hid[...], weight[...], preferred_element_type=F32)
+    halves = [pl.ds(half * TILE, TILE) for half in range(2)]
+    for half, rows in enumerate(halves):
+        hx[x, rows, :] = partial[half * TILE:(half + 1) * TILE, :].astype(BF)
+
+        @pl.when(home != x)
+        def _(half=half, rows=rows):
+            start(hx.at[x, rows], hx.at[x, rows], hx_sent, hx_recv.at[half * NX + x],
+                  at(home, y, z, k))
+
+    def middle(rows):
+        v = jnp.dot(hid[rows, :], weight[...], preferred_element_type=F32)
         s = 1.0 / (1.0 + jnp.exp(-v))
-        slope_ref[...] = (cotangent[...].astype(F32) * (s * (1.0 + v * (1.0 - s)))).astype(BF)
-        act_ref[...] = (v * s).astype(BF)
+        slope = cotangent[rows, :].astype(F32) * (s * (1.0 + v * (1.0 - s)))
+        slope_ref[rows, :] = slope.astype(BF)
+        act_ref[rows, :] = (v * s).astype(BF)
 
     @pl.when(me.source)
     def _():
-        def take(d):
-            wait(hx.at[(x + d) % NX], hx_recv.at[(x + d) % NX])
-
-        loop(1, NX, take)
-        hidden = (hx[0].astype(F32) + hx[1].astype(F32)) + (hx[2].astype(F32) + hx[3].astype(F32))
-        hid[...] = hidden.astype(BF)
-        middle()
-        pan2[me.panel] = slope_ref[0:TILE, :]
-        pan2[HALF + me.panel] = slope_ref[TILE:, :]
-
-    two.begin()
-
-    @pl.when(me.source)
-    def _():
+        for half, rows in enumerate(halves):
+            def take(d, half=half, rows=rows):
+                other = (x + d) % NX
+                wait(hx.at[other, rows], hx_recv.at[half * NX + other])
+
+            loop(1, NX, take)
+            terms = [hx[j, rows, :].astype(F32) for j in range(NX)]
+            hid[rows, :] = ((terms[0] + terms[1]) + (terms[2] + terms[3])).astype(BF)
+            middle(rows)
+            pan2[half * HALF + me.panel] = slope_ref[rows, :]
+            two.root(range(half, 2 * PARTS, 2))
+        two.mate()
+
         def tell(d):
             start(hid, hid, hx_sent, hid_recv, at((x + d) % NX, y, z, k))
 
@@ -282,7 +299,8 @@
     @pl.when(jnp.logical_not(me.source))
     def _():
         wait(hid, hid_recv)
-        middle()
+        for rows in halves:
+            middle(rows)
 
     term = lax.dot_general(hid[...], slope_ref[...], (((0,), (0,)), ((), ())),
                            preferred_element_type=F32)
@@ -390,7 +408,7 @@
     loop(0, 6, lambda i: wait(bp.at[0], b_sent))
 
 
-CUTS = (0.3, 0.55, 0.8)
+CUTS = (0.2, 0.5, 0.8)
 
 
 def write_out(act, grad, wg, act_out, grad_out, wg_out, sems):
@@ -443,7 +461,7 @@
             pltpu.VMEM((NX, 64, F), BF),
             dma((2,)), dma(()), dma(()), dma(()), dma(()),
             dma((2 * PARTS * HALF,)), dma((2 * PARTS * HALF,)), dma(()), dma(()), dma(()), dma(()),
-            dma((NX,)), dma(()), dma(()),
+            dma((2 * NX,)), dma(()), dma(()),
             dma((16,)), dma((NZ,)), dma((16,)), dma((NX,)), dma(()), dma(()),
             dma((NX,)), dma((NX,)), dma(()),
         ],

time: 83.3 us -> 80.1 us (0.962)
  Pallas kernels: 81.9 us -> 79.1 us
    pallas_call x1, Pallas kernels: 81.1 us -> 78.3 us  [on_device(): pl.pallas_call(kernel, out_shape=(pltpu.VMEM((ROWS, F), BF), pltpu.VMEM((...]
where the time goes in v4:
time: 80.1 us; the launch traced here: 79.8 us
  Pallas kernels  79.1 us (99%)
    pallas_call x1, Pallas kernels, on_device(): pl.pallas_call(kernel, out_shape=(pltpu.VMEM((ROWS, F), BF), pltpu.VMEM((...  78.3 us

profile of v4, /device:TPU:1, one launch (start us, length us, event | category | flops | bytes accessed | tf_op | source)
XLA Modules:
  0.0 79.8 jit_solution(2019841341808803580)
XLA Ops:
  0.6 78.3 %graph_layer.1 = (bf16[256,256]{1,0:T(8,128)(2,1)S(1)}, bf16[256,256]{1,0:T(8,128)(2,1)S(1)}, f32[256,256]{1,0:T(8,128)S(1)}) custom-call(bf16[256,256]{1,0:T(8,128)(2,1)} %features.1, bf16[256,256]{1,0:T(8,128)(2,1)} %weight_in.1, bf16[256,256]{1,0:T(8,128)(2,1)} %cotangent_in.1, s32[1,1,2,20]{3,2,1,0:T(2,128)} %bitcast.1, ...), custom_call_target="tpu_custom_call" | custom-call | tf_op jit(solution)/shard_map/graph_layer/pallas_call | solution.py:438
  78.9 0.8 %write_out.1 = (bf16[256,256]{1,0:T(8,128)(2,1)}, bf16[256,256]{1,0:T(8,128)(2,1)}, f32[256,256]{1,0:T(8,128)}) custom-call(bf16[256,256]{1,0:T(8,128)(2,1)S(1)} %get-tuple-element.6.act, bf16[256,256]{1,0:T(8,128)(2,1)S(1)} %get-tuple-element.7.grad, f32[256,256]{1,0:T(8,128)S(1)} %get-tuple-element.8.wg), custom_call_target="tpu_custom_call" | custom-call | tf_op jit(solution)/shard_map/write_out/pallas_call | solution.py:473

commit v5 on v4

--- a/solution.py
+++ b/solution.py
@@ -182,9 +182,9 @@
 
 def kernel(features, weight_in, cotangent_in, coords_in, tiles_in, act_ref, grad_ref, wg_ref,
            coords, pan1, pan2, weight, cotangent, tiles, lhs, rhs, hx, hid, slope_ref,
-           wgp, wy, wz, wall, bp, bx, ig,
+           wgp, ws, wt, wy, wz, wall, bp, bx, ig,
            f_sem, w_sem, c_sem, t_sem, i_sem, recv1, recv2, sent1, sent2, pair1, pair2, hx_recv, hx_sent, hid_recv,
-           wy_recv, wz_recv, wq_recv, wx_recv, w_sent, wx_sent, bx_recv, ig_recv, b_sent):
+           ws_recv, ws_sent, wy_recv, wz_recv, wq_recv, wx_recv, w_sent, wx_sent, bx_recv, ig_recv, b_sent):
     me = Place()
     x, y, z, k = me.x, me.y, me.z, me.k
 
@@ -292,7 +292,8 @@
         def tell(d):
             start(hid, hid, hx_sent, hid_recv, at((x + d) % NX, y, z, k))
 
-        loop(1, NX, tell)
+        for d in (2, 1, 3):
+            tell(d)
 
     two.forward(0, CUTS[0])
 
@@ -302,29 +303,35 @@
         for rows in halves:
             middle(rows)
 
-    term = lax.dot_general(hid[...], slope_ref[...], (((0,), (0,)), ((), ())),
-                           preferred_element_type=F32)
-    wgp[0] = term[:, 0:TILE]
-    wgp[1] = term[:, TILE:]
-    mine = y * 2 + k
-
-    def chunk(to):
-        return wgp.at[to % 2, pl.ds(pl.multiple_of(x * 64 + (to // 2) * 8, 8), 8), :]
+    def begin_term():
+        term = lax.dot_general(hid[...], slope_ref[...], (((0,), (0,)), ((), ())),
+                               preferred_element_type=F32)
+        wgp[0] = term[:, 0:TILE]
+        wgp[1] = term[:, TILE:]
+        start(wgp.at[1 - k, rows64], ws, ws_sent, ws_recv.at[0], at(x, y, z, 1 - k))
+
+    rows64 = pl.ds(pl.multiple_of(x * 64, 64), 64)
+    begin_term()
+
+    two.forward(CUTS[0], CUTS[1])
+
+    wait(ws, ws_recv.at[0])
+    wt[...] = (wgp[k, rows64, :] + ws[...]).reshape(NY, 8, TILE)
 
     def scatter_y(d):
-        to = (mine + d) % 16
-        start(chunk(to), wy.at[mine], w_sent, wy_recv.at[mine], at(x, to // 2, z, to % 2))
-
-    loop(1, 16, scatter_y)
-    wy[mine] = chunk(mine)[...]
-
-    two.forward(CUTS[0], CUTS[1])
+        to = (y + d) % NY
+        start(wt.at[to], wy.at[y], w_sent, wy_recv.at[y], at(x, to, z, k))
+
+    loop(1, NY, scatter_y)
+    wy[y] = wt[y]
+
+    two.forward(CUTS[1], CUTS[2])
 
     def take_y(d):
-        src = (mine + d) % 16
+        src = (y + d) % NY
         wait(wy.at[src], wy_recv.at[src])
 
-    loop(1, 16, take_y)
+    loop(1, NY, take_y)
     wz[z] = jnp.sum(wy[...], axis=0)
 
     def scatter_z(d):
@@ -332,23 +339,21 @@
 
     loop(1, NZ, scatter_z)
 
-    two.forward(CUTS[1], CUTS[2])
+    two.forward(CUTS[2], CUTS[3])
 
     def take_z(d):
         src = (z + d) % NZ
         wait(wz.at[src], wz_recv.at[src])
 
     loop(1, NZ, take_z)
-    wall[x, mine] = jnp.sum(wz[...], axis=0) * (1.0 / math.sqrt(ROWS * NY * NZ * 2))
+    wall[k, x, y] = jnp.sum(wz[...], axis=0) * (1.0 / math.sqrt(ROWS * NY * NZ * 2))
 
     def spread_y(d):
-        to = (mine + d) % 16
-        start(wall.at[x, mine], wall.at[x, mine], w_sent, wq_recv.at[mine],
-              at(x, to // 2, z, to % 2))
-
-    loop(1, 16, spread_y)
-
-    two.forward(CUTS[2], 1)
+        start(wall.at[k, x, y], wall.at[k, x, y], w_sent, wq_recv.at[y], at(x, (y + d) % NY, z, k))
+
+    loop(1, NY, spread_y)
+
+    two.forward(CUTS[3], 1)
     two.finish()
 
     bp[...] = aggregate(coords, lhs, pan2, rhs).astype(BF).reshape(NX, 64, F)
@@ -357,19 +362,21 @@
         to = (x + d) % NX
         start(bp.at[to], bx.at[x], b_sent, bx_recv.at[x], at(to, y, z, k))
 
-    loop(1, NX, give_back)
+    for d in (2, 1, 3):
+        give_back(d)
     bx[x] = bp[x]
 
     def take_q(d):
-        src = (mine + d) % 16
-        wait(wall.at[x, src], wq_recv.at[src])
-
-    loop(1, 16, take_q)
+        src = (y + d) % NY
+        wait(wall.at[k, x, src], wq_recv.at[src])
+
+    loop(1, NY, take_q)
 
     def spread_x(d):
-        start(wall.at[x], wall.at[x], wx_sent, wx_recv.at[x], at((x + d) % NX, y, z, k))
-
-    loop(1, NX, spread_x)
+        start(wall.at[k, x], wall.at[k, x], wx_sent, wx_recv.at[x], at((x + d) % NX, y, z, k))
+
+    for d in (2, 1, 3):
+        spread_x(d)
 
     def take_back(d):
         wait(bx.at[(x + d) % NX], bx_recv.at[(x + d) % NX])
@@ -382,33 +389,37 @@
     def give_grad(d):
         start(ig.at[x], ig.at[x], b_sent, ig_recv.at[x], at((x + d) % NX, y, z, k))
 
-    loop(1, NX, give_grad)
+    for d in (2, 1, 3):
+        give_grad(d)
+
+    def take_x(d):
+        wait(wall.at[k, (x + d) % NX], wx_recv.at[(x + d) % NX])
+
+    loop(1, NX, take_x)
+    start(wall.at[k], wall.at[k], ws_sent, ws_recv.at[1], at(x, y, z, 1 - k))
 
     one.end()
     two.end()
     loop(0, jnp.where(me.source, NX - 1, 1), lambda d: wait(hx.at[0], hx_sent))
-    loop(0, 15 + 7 + 15, lambda i: wait(wz.at[0], w_sent))
-
-    def take_x(d):
-        wait(wall.at[(x + d) % NX], wx_recv.at[(x + d) % NX])
-
-    loop(1, NX, take_x)
-    for quarter in range(NX):
-        for row in range(8):
-            for half in range(2):
-                wg_ref[quarter * 64 + row * 8:quarter * 64 + row * 8 + 8,
-                       half * TILE:(half + 1) * TILE] = wall[quarter, row * 2 + half]
+    loop(0, 7 + 7 + 7, lambda i: wait(wz.at[0], w_sent))
 
     def take_grad(d):
         wait(ig.at[(x + d) % NX], ig_recv.at[(x + d) % NX])
 
     loop(1, NX, take_grad)
     grad_ref[...] = ig[...].reshape(ROWS, F)
-    loop(1, NX, lambda d: wait(wall.at[0], wx_sent))
+    wait(wall.at[1 - k], ws_recv.at[1])
+    for half in range(2):
+        for quarter in range(NX):
+            wg_ref[quarter * 64:quarter * 64 + 64, half * TILE:(half + 1) * TILE] = (
+                wall[half, quarter].reshape(64, TILE))
+    loop(1, NX, lambda d: wait(wall.at[0, 0], wx_sent))
+    wait(ws, ws_sent)
+    wait(wall.at[0], ws_sent)
     loop(0, 6, lambda i: wait(bp.at[0], b_sent))
 
 
-CUTS = (0.2, 0.5, 0.8)
+CUTS = (0.2, 0.3, 0.55, 0.85)
 
 
 def write_out(act, grad, wg, act_out, grad_out, wg_out, sems):
@@ -453,16 +464,18 @@
             pltpu.VMEM((ROWS, F), BF),
             pltpu.VMEM((ROWS, F), BF),
             pltpu.VMEM((2, F, TILE), F32),
-            pltpu.VMEM((16, 8, TILE), F32),
+            pltpu.VMEM((64, TILE), F32),
+            pltpu.VMEM((NY, 8, TILE), F32),
+            pltpu.VMEM((NY, 8, TILE), F32),
             pltpu.VMEM((NZ, 8, TILE), F32),
-            pltpu.VMEM((NX, 16, 8, TILE), F32),
+            pltpu.VMEM((2, NX, NY, 8, TILE), F32),
             pltpu.VMEM((NX, 64, F), BF),
             pltpu.VMEM((NX, 64, F), BF),
             pltpu.VMEM((NX, 64, F), BF),
             dma((2,)), dma(()), dma(()), dma(()), dma(()),
             dma((2 * PARTS * HALF,)), dma((2 * PARTS * HALF,)), dma(()), dma(()), dma(()), dma(()),
             dma((2 * NX,)), dma(()), dma(()),
-            dma((16,)), dma((NZ,)), dma((16,)), dma((NX,)), dma(()), dma(()),
+            dma((2,)), dma(()), dma((NY,)), dma((NZ,)), dma((NY,)), dma((NX,)), dma(()), dma(()),
             dma((NX,)), dma((NX,)), dma(()),
         ],
         compiler_params=pltpu.CompilerParams(

time: 80.1 us -> 79.4 us (level)
  no operation moved by 1% of the time
where the time goes in v5:
time: 79.4 us; the launch traced here: 79.3 us
  Pallas kernels  78.7 us (99%)
    pallas_call x1, Pallas kernels, on_device(): pl.pallas_call(kernel, out_shape=(pltpu.VMEM((ROWS, F), BF), pltpu.VMEM((...  77.8 us

profile of v5, /device:TPU:1, one launch (start us, length us, event | category | flops | bytes accessed | tf_op | source)
XLA Modules:
  0.0 79.3 jit_solution(1600233518207607676)
XLA Ops:
  0.6 77.8 %graph_layer.1 = (bf16[256,256]{1,0:T(8,128)(2,1)S(1)}, bf16[256,256]{1,0:T(8,128)(2,1)S(1)}, f32[256,256]{1,0:T(8,128)S(1)}) custom-call(bf16[256,256]{1,0:T(8,128)(2,1)} %features.1, bf16[256,256]{1,0:T(8,128)(2,1)} %weight_in.1, bf16[256,256]{1,0:T(8,128)(2,1)} %cotangent_in.1, s32[1,1,2,20]{3,2,1,0:T(2,128)} %bitcast.1, ...), custom_call_target="tpu_custom_call" | custom-call | tf_op jit(solution)/shard_map/graph_layer/pallas_call | solution.py:449
  78.5 0.8 %write_out.1 = (bf16[256,256]{1,0:T(8,128)(2,1)}, bf16[256,256]{1,0:T(8,128)(2,1)}, f32[256,256]{1,0:T(8,128)}) custom-call(bf16[256,256]{1,0:T(8,128)(2,1)S(1)} %get-tuple-element.6.act, bf16[256,256]{1,0:T(8,128)(2,1)S(1)} %get-tuple-element.7.grad, f32[256,256]{1,0:T(8,128)S(1)} %get-tuple-element.8.wg), custom_call_target="tpu_custom_call" | custom-call | tf_op jit(solution)/shard_map/write_out/pallas_call | solution.py:486

commit v6 on v5

--- a/solution.py
+++ b/solution.py
@@ -274,6 +274,14 @@
         slope_ref[rows, :] = slope.astype(BF)
         act_ref[rows, :] = (v * s).astype(BF)
 
+    def begin_term():
+        term = lax.dot_general(hid[...], slope_ref[...], (((0,), (0,)), ((), ())),
+                               preferred_element_type=F32)
+        wgp[0] = term[:, 0:TILE]
+        wgp[1] = term[:, TILE:]
+        start(wgp.at[1 - k, rows64], ws, ws_sent, ws_recv.at[0], at(x, y, z, 1 - k))
+
+    rows64 = pl.ds(pl.multiple_of(x * 64, 64), 64)
     @pl.when(me.source)
     def _():
         for half, rows in enumerate(halves):
@@ -287,13 +295,13 @@
             middle(rows)
             pan2[half * HALF + me.panel] = slope_ref[rows, :]
             two.root(range(half, 2 * PARTS, 2))
-        two.mate()
-
         def tell(d):
             start(hid, hid, hx_sent, hid_recv, at((x + d) % NX, y, z, k))
 
         for d in (2, 1, 3):
             tell(d)
+        two.mate()
+        begin_term()
 
     two.forward(0, CUTS[0])
 
@@ -302,16 +310,8 @@
         wait(hid, hid_recv)
         for rows in halves:
             middle(rows)
-
-    def begin_term():
-        term = lax.dot_general(hid[...], slope_ref[...], (((0,), (0,)), ((), ())),
-                               preferred_element_type=F32)
-        wgp[0] = term[:, 0:TILE]
-        wgp[1] = term[:, TILE:]
-        start(wgp.at[1 - k, rows64], ws, ws_sent, ws_recv.at[0], at(x, y, z, 1 - k))
-
-    rows64 = pl.ds(pl.multiple_of(x * 64, 64), 64)
-    begin_term()
+        begin_term()
+
 
     two.forward(CUTS[0], CUTS[1])
 

time: 79.4 us -> 79.6 us (level)
  no operation moved by 1% of the time
where the time goes in v6:
time: 79.6 us; the launch traced here: 79.4 us
  Pallas kernels  78.8 us (99%)
    pallas_call x1, Pallas kernels, on_device(): pl.pallas_call(kernel, out_shape=(pltpu.VMEM((ROWS, F), BF), pltpu.VMEM((...  78 us

profile of v6, /device:TPU:1, one launch (start us, length us, event | category | flops | bytes accessed | tf_op | source)
XLA Modules:
  0.0 79.4 jit_solution(6347380552962718260)
XLA Ops:
  0.6 78.0 %graph_layer.1 = (bf16[256,256]{1,0:T(8,128)(2,1)S(1)}, bf16[256,256]{1,0:T(8,128)(2,1)S(1)}, f32[256,256]{1,0:T(8,128)S(1)}) custom-call(bf16[256,256]{1,0:T(8,128)(2,1)} %features.1, bf16[256,256]{1,0:T(8,128)(2,1)} %weight_in.1, bf16[256,256]{1,0:T(8,128)(2,1)} %cotangent_in.1, s32[1,1,2,20]{3,2,1,0:T(2,128)} %bitcast.1, ...), custom_call_target="tpu_custom_call" | custom-call | tf_op jit(solution)/shard_map/graph_layer/pallas_call | solution.py:449
  78.6 0.8 %write_out.1 = (bf16[256,256]{1,0:T(8,128)(2,1)}, bf16[256,256]{1,0:T(8,128)(2,1)}, f32[256,256]{1,0:T(8,128)}) custom-call(bf16[256,256]{1,0:T(8,128)(2,1)S(1)} %get-tuple-element.6.act, bf16[256,256]{1,0:T(8,128)(2,1)S(1)} %get-tuple-element.7.grad, f32[256,256]{1,0:T(8,128)S(1)} %get-tuple-element.8.wg), custom_call_target="tpu_custom_call" | custom-call | tf_op jit(solution)/shard_map/write_out/pallas_call | solution.py:486
